TPU v7x, 128 devices: a whole 4x4x4 slice. The times are simulated.
128 devices in a mesh: rows: 32 (over x, y, core), rep: 4 (over z).
Axes of the slice: x: 4, y: 4, z: 4, core: 2. Of those that a mesh axis runs over, the one named last changes fastest.
Arguments:
- features: float32 [32768, 602], P(('rows', 'rep')), may hold values from -6 to 6
- weight: float32 [602, 512], replicated, may hold values from -0.25 to 0.25
- cotangent: float32 [32768, 512], P(('rows', 'rep')), may hold values from -4 to 4
- tile_values: float32 [4096, 128, 128], P(('rows', 'rep')), may hold values from -0.1875 to 0.1875
- tile_row: int32 [4096], P(('rows', 'rep')), may hold values from 0 to 7
- tile_col: int32 [4096], P(('rows', 'rep')), may hold values from 0 to 63
- tile_count: int32 [128], P(('rows', 'rep')), may hold values from 8 to 32, as said below
Outputs:
- activated: float32 [32768, 512], P(('rows', 'rep'))
- grad_features: float32 [32768, 602], P(('rows', 'rep'))
- grad_weight: float32 [602, 512], replicated
Inputs may be any that keep to these rules, and one draw needn't show every extreme that they name: `tile_count`: slots at or beyond a device's count hold no tile; some device has all 32 slots live.
All inputs are finite; a program needn't handle non-finite values.
Results may differ from a plain program's by a relative error of at most 0.0003.
Values sent between devices are 32-bit elements; how exact they have to be, the bound alone decides.
A program may use at most 128 MiB of HBM per device.

v0:
```python
import jax
import jax.numpy as jnp
from jax import lax
from jax.sharding import PartitionSpec as P

BLOCK = 128


def slot_term(source, values, take_index, put_index, alive, targets, pattern):
    highest = lax.Precision.HIGHEST
    picked = source[take_index]
    product = jnp.einsum(pattern, values, picked, precision=highest)
    product = product * alive.astype(jnp.float32)[:, None, None]
    empty = jnp.zeros((targets, product.shape[1], product.shape[2]), jnp.float32)
    return empty.at[put_index].add(product)


def slot_product(source, values, take_index, put_index, live_count, targets, pattern):
    width = source.shape[-1]
    alive = jnp.arange(values.shape[0], dtype=jnp.int32) < live_count
    total = slot_term(source, values, take_index, put_index, alive, targets, pattern)
    return total.reshape(targets * BLOCK, width)


def body(features, weight, cotangent, tile_values, tile_row, tile_col, tile_count):
    highest = lax.Precision.HIGHEST
    per_device = features.shape[0] // BLOCK
    groups = lax.axis_size("rep") * per_device
    columns = lax.axis_size("rows") * per_device
    live_count = tile_count[0]
    gathered = lax.all_gather(features, "rows", axis=0, tiled=True)
    partial_value = slot_product(
        gathered.reshape(columns, BLOCK, -1),
        tile_values,
        tile_col,
        tile_row,
        live_count,
        groups,
        "tij,tjh->tih",
    )
    aggregated = lax.psum_scatter(partial_value, "rep", scatter_dimension=0, tiled=True)
    summed = jnp.dot(aggregated, weight, precision=highest, preferred_element_type=jnp.float32)
    sigma = jax.nn.sigmoid(summed)
    activated = summed * sigma
    grad_pre = cotangent * sigma * (1.0 + summed * (1.0 - sigma))
    group_grads = lax.all_gather(grad_pre, "rep", axis=0, tiled=True)
    column_part = slot_product(
        group_grads.reshape(groups, BLOCK, -1),
        tile_values,
        tile_row,
        tile_col,
        live_count,
        columns,
        "tij,tih->tjh",
    )
    propagated = lax.psum_scatter(column_part, "rows", scatter_dimension=0, tiled=True)
    local_weight = jnp.dot(
        features.T, propagated, precision=highest, preferred_element_type=jnp.float32
    )
    grad_weight = lax.psum(local_weight, ("rows", "rep"))
    grad_features = jnp.dot(
        propagated, weight.T, precision=highest, preferred_element_type=jnp.float32
    )
    return (activated, grad_features, grad_weight)


def solution(mesh):
    in_specs = (
        P(("rows", "rep"), None),
        P(),
        P(("rows", "rep"), None),
        P(("rows", "rep"), None, None),
        P(("rows", "rep")),
        P(("rows", "rep")),
        P(("rows", "rep")),
    )
    out_specs = (P(("rows", "rep"), None), P(("rows", "rep"), None), P())
    return jax.shard_map(body, mesh=mesh, in_specs=in_specs, out_specs=out_specs, check_vma=False)
```

profile of v0, /device:TPU:1, one launch (start us, length us, event | category | flops | bytes accessed | tf_op | source)
XLA Modules:
  0.0 596.1 jit_solution(6078725450716095511)
XLA Ops:
  7.2 0.0 all-gather.3.cloned.1.call-start
  7.2 0.7 all-gather.3.cloned.1.call-update
  7.9 0.0 reduce-scatter.3.cloned.1.call-start
  8.6 0.7 compare_select_fusion
  9.3 0.7 compare_select_fusion.1
  9.9 93.1 %all-gather.3.cloned.1.call-done = f32[8192,602]{0,1:T(8,128)} async-done(((f32[256,602]{0,1:T(8,128)}), f32[8192,602]{0,1:T(8,128)}) %all-gather.3.cloned.1.call-update) | async-done | bytes 19726352 | tf_op jit(solution)/shard_map/all_gather | solution.py:31
  103.1 10.7 %copy.19 = f32[76,8,64,128]{3,2,1,0:T(8,128)S(1)} copy(f32[76,8,64,128]{3,1,2,0:T(8,128)} %bitcast.36) | data formatting | bytes 39845888
  113.8 7.0 %slice_bitcast_fusion = f32[64,128,602]{1,0,2:T(8,128)} fusion(f32[608,64,128]{2,1,0:T(8,128)S(1)} %bitcast.34), kind=kLoop, calls=%fused_computation.4 | loop fusion | bytes 39452672 | tf_op jit(solution)/shard_map/reshape | solution.py:33
  120.8 20.7 %copy.14 = f32[64,128,602]{1,2,0:T(8,128)} copy(f32[64,128,602]{1,0,2:T(8,128)} %slice_bitcast_fusion) | data formatting | bytes 39452672 | tf_op jit(solution)/shard_map/reshape | solution.py:33
  141.5 11.6 %gather_fusion = f32[32,128,602]{1,2,0:T(8,128)} fusion(f32[64,128,602]{1,2,0:T(8,128)} %copy.14, s32[1024]{0:T(1024)S(1)} %pad_clamp_fusion.1), kind=kCustom, calls=%fused_computation | custom fusion | bytes 19726464 | tf_op jit(solution)/shard_map/gather | solution.py:11
  153.0 12.6 %multiply_bitcast_fusion = f32[32,128,602]{1,2,0:T(8,128)} fusion(f32[32]{0:T(128)S(1)} %compare_convert_fusion, f32[32,128,602]{1,2,0:T(8,128)} %gather_fusion, f32[32,128,128]{2,1,0:T(8,128)S(1)} %copy-done), kind=kOutput, calls=%fused_computation.5 | convolution fusion | flops 3789922304 | bytes 21823616 | tf_op jit(solution)/shard_map/tij,tjh->tih/dot_general | solution.py:12
  165.7 1.6 broadcast_in_dim.16
  167.3 20.0 %scatter_fusion = f32[8,128,602]{1,2,0:T(8,128)} fusion(f32[8,128,602]{1,2,0:T(8,128)} %broadcast_in_dim.16, s32[32]{0:T(128)S(1)} %compare_select_fusion.1, f32[32,128,602]{1,2,0:T(8,128)} %multiply_bitcast_fusion), kind=kCustom, calls=%fused_computation.2 | custom fusion | flops 2465792 | bytes 29589632 | tf_op jit(solution)/shard_map/scatter-add | solution.py:15
  187.3 3.2 copy.22
  190.6 0.2 pad.2
  190.7 2.0 copy.20
  192.8 0.0 all-gather.5.cloned.1.call-start
  192.8 33.4 %reduce-scatter.3.cloned.1.call-done = f32[256,602]{0,1:T(8,128)} async-done(((f32[1024,602]{0,1:T(8,128)}), f32[256,602]{0,1:T(8,128)}) %reduce-scatter.3.cloned.1.call-update) | async-done | bytes 616464 | tf_op jit(solution)/shard_map/reduce_scatter | solution.py:41
  226.2 3.8 add_multiply_fusion
  230.1 0.0 reduce-scatter.5.cloned.1.call-start
  230.1 30.7 %all-gather.5.cloned.1.call-done = f32[1024,512]{1,0:T(8,128)} async-done(((f32[256,512]{1,0:T(8,128)}), f32[1024,512]{1,0:T(8,128)}) %all-gather.5.cloned.1.call-update) | async-done | bytes 2097168 | tf_op jit(solution)/shard_map/all_gather | solution.py:46
  260.8 5.9 gather_fusion.1
  266.7 17.3 %multiply_bitcast_fusion.1 = f32[32,128,512]{1,2,0:T(8,128)} fusion(f32[32]{0:T(128)S(1)} %compare_convert_fusion, f32[32,128,512]{2,1,0:T(8,128)} %gather_fusion.1, f32[32,128,128]{2,1,0:T(8,128)S(1)} %copy-done), kind=kOutput, calls=%fused_computation.6 | convolution fusion | flops 3223322624 | bytes 18874496 | tf_op jit(solution)/shard_map/tij,tih->tjh/dot_general | solution.py:12
  284.0 9.0 %copy.17 = f32[32,128,512]{2,1,0:T(8,128)} copy(f32[32,128,512]{1,2,0:T(8,128)} %multiply_bitcast_fusion.1) | data formatting | bytes 16777216 | tf_op jit(solution)/shard_map/mul | solution.py:13
  293.0 7.9 %broadcast_in_dim.19 = f32[64,128,512]{2,1,0:T(8,128)} broadcast(f32[]{:T(128)} %constant.5.clone.1), dimensions={} | broadcast | bytes 16777220 | tf_op jit(solution)/shard_map/broadcast_in_dim | solution.py:14
  300.9 18.8 %scatter_fusion.1 = f32[64,128,512]{2,1,0:T(8,128)} fusion(f32[64,128,512]{2,1,0:T(8,128)} %broadcast_in_dim.19, s32[32]{0:T(128)S(1)} %compare_select_fusion, f32[32,128,512]{2,1,0:T(8,128)} %copy.17), kind=kCustom, calls=%fused_computation.3 | custom fusion | flops 2097152 | bytes 25165952 | tf_op jit(solution)/shard_map/scatter-add | solution.py:15
  319.7 0.3 all-reduce.2.cloned.1.call-start
  320.0 113.5 %reduce-scatter.5.cloned.1.call-done = f32[256,512]{1,0:T(8,128)} async-done(((f32[8192,512]{1,0:T(8,128)}), f32[256,512]{1,0:T(8,128)}) %reduce-scatter.5.cloned.1.call-update) | async-done | bytes 524304 | tf_op jit(solution)/shard_map/reduce_scatter | solution.py:56
  433.4 3.5 convolution_bitcast_fusion
  436.9 3.0 fusion.1
  440.0 147.2 %all-reduce.2.cloned.1.call-done = f32[602,512]{1,0:T(8,128)} async-done(((f32[602,512]{1,0:T(8,128)}), f32[602,512]{1,0:T(8,128)}) %all-reduce.2.cloned.1.call-update) | async-done | bytes 1232912 | tf_op jit(solution)/shard_map/psum | solution.py:60
  587.2 2.4 copy.27
  (11 shorter events, 0.1 us)
Async XLA Ops:
  7.2 145.9 %copy-start = (f32[32,128,128]{2,1,0:T(8,128)S(1)}, f32[32,128,128]{2,1,0:T(8,128)}, u32[]{:S(2)}) copy-start(f32[32,128,128]{2,1,0:T(8,128)} %param.10) | copy-start | bytes 6291460
  7.2 95.9 %all-gather.3.cloned.1.call-start = ((), (), s32[]{:S(2)}) async-start(), calls=%async_computation.2 | async-start | bytes 20545536 | tf_op jit(solution)/shard_map/all_gather | solution.py:31
  7.9 218.3 %reduce-scatter.3.cloned.1.call-start = ((), (), s32[]{:S(2)}) async-start(), calls=%async_computation.3 | async-start | bytes 3112960 | tf_op jit(solution)/shard_map/reduce_scatter | solution.py:41
  187.3 38.9 %copy-start.1 = (f32[602,512]{1,0:T(8,128)S(1)}, f32[602,512]{1,0:T(8,128)}, u32[]{:S(2)}) copy-start(f32[602,512]{1,0:T(8,128)} %param.8) | copy-start | bytes 3698692
  192.8 68.0 %all-gather.5.cloned.1.call-start = ((), (), s32[]{:S(2)}) async-start(), calls=%async_computation.4 | async-start | bytes 2621440 | tf_op jit(solution)/shard_map/all_gather | solution.py:46
  230.1 203.4 %reduce-scatter.5.cloned.1.call-start = ((), (), s32[]{:S(2)}) async-start(), calls=%async_computation.5 | async-start | bytes 17301504 | tf_op jit(solution)/shard_map/reduce_scatter | solution.py:56
  319.7 267.5 %all-reduce.2.cloned.1.call-start = ((), (), s32[]{:S(2)}) async-start(), calls=%async_computation.6 | async-start | bytes 2490368 | tf_op jit(solution)/shard_map/psum | solution.py:60
Sparse Core Ops, SparseCore 0:
  10.2 92.8 all-gather.2
  192.9 33.2 reduce-scatter.2
  230.2 30.5 all-gather.4
  319.8 113.5 reduce-scatter.4
  438.7 148.4 all-reduce.1
where the time goes:
time: 597 us; the launch traced here: 596 us
  waiting for transfers between devices  419 us (70%)
  local copies, waits for them, and re-layouts  82.2 us (14%)
  matrix products  40.3 us (7%)
  other arithmetic  40.2 us (7%)
  between operations  14.5 us (2%)
    psum x1, waiting for transfers between devices, body(): grad_weight = lax.psum(local_weight, ('rows', 'rep'))  147 us
    reduce_scatter x1, waiting for transfers between devices, body(): lax.psum_scatter(column_part, 'rows', scatter_dimension=0, tiled=True)  113 us
    all_gather x1, waiting for transfers between devices, body(): gathered = lax.all_gather(features, 'rows', axis=0, tiled=True)  93.1 us
    scatter-add x2, other arithmetic, slot_term(): return empty.at[put_index].add(product)  38.8 us
    reduce_scatter x1, waiting for transfers between devices, body(): lax.psum_scatter(partial_value, 'rep', scatter_dimension=0, tiled=True)  33.4 us
    all_gather x1, waiting for transfers between devices, body(): group_grads = lax.all_gather(grad_pre, 'rep', axis=0, tiled=True)  30.7 us
    dot_general x2, matrix products, slot_term(): product = jnp.einsum(pattern, values, picked, precision=highest)  29.9 us
    reshape x2, local copies, waits for them, and re-layouts, body(): gathered.reshape(columns, BLOCK, -1)  27.6 us
  transfers between devices with their start and end apart: 5, of which 5 were waited for; matrix products, arithmetic and copies ran while one was open for 1% of the time, Pallas kernels for 0%

commit v1 on v0

v1 whole, which is shorter than its diff:
```python
import functools

import jax
import jax.numpy as jnp
from jax import lax
from jax.experimental import pallas as pl
from jax.experimental.pallas import tpu as pltpu
from jax.sharding import PartitionSpec as P

MESH = pl.DeviceIdType.MESH
F32 = jnp.float32
BF16 = jnp.bfloat16

BLOCK = 128
HALF = BLOCK // 2
SLOTS = 32
CHUNKS = 4
SIDE = 4
PAD = 640
COPIES = 69 * CHUNKS

ROWS, COLS = 8, 64
ROW_PREV, ROW_LAST, COL_PREV, COL_LAST = 0, SLOTS, SLOTS + ROWS, 2 * SLOTS + ROWS

LO, HI = pl.ds(0, HALF), pl.ds(HALF, HALF)


def split(value):
    high = value.astype(BF16)
    return high, (value - high.astype(F32)).astype(BF16)


def mm(a, b):
    left = jnp.concatenate([a[0], a[1], a[0]], axis=1)
    right = jnp.concatenate([b[0], b[0], b[1]], axis=0)
    return jnp.dot(left, right, preferred_element_type=F32)


def mm_nt(a, b):
    left = jnp.concatenate([a[0], a[1], a[0]], axis=1)
    right = jnp.concatenate([b[0], b[0], b[1]], axis=1)
    return lax.dot_general(left, right, (((1,), (1,)), ((), ())), preferred_element_type=F32)


def kernel(*refs):
    C = CHUNKS
    row_ref, col_ref, live_ref, f_hbm, w_hbm, cot_hbm, tiles_hbm, act_ref, gf_ref, gw_ref = refs[:10]
    refs = list(refs[10:])

    def take(count):
        out = refs[:count]
        del refs[:count]
        return out

    G, R0, part, zfin, GG = (take(C) for _ in range(5))
    m1, f1, m2, f2 = (take(C) for _ in range(4))
    gwl, sb, zb, xb, yb, gwo = (take(C) for _ in range(6))
    slots, tiles, tiles_t, w_raw, w_pad, f_raw, cot, f_hi, f_lo, ft_hi, ft_lo, prop, gf_acc, plan = take(14)
    send_sem, recv_sem, load_sem = take(3)
    W = prop.shape[1] // C

    r = lax.axis_index("rows")
    z = lax.axis_index("rep")
    x, y, p = r // 8, (r // 2) % 4, r % 2
    q = 1 - p

    def at(i, d):
        return (i + d) % SIDE

    def dev(dx=0, dy=0, dz=0, core=None):
        c = p if core is None else core
        return (at(x, dx) * 8 + at(y, dy) * 2 + c, at(z, dz))

    xl, xr, xo = at(x, 3), at(x, 1), at(x, 2)
    yl, yr, yo = at(y, 3), at(y, 1), at(y, 2)
    zl, zr, zo = at(z, 3), at(z, 1), at(z, 2)
    XR, XL, YR, YL, ZR, ZL = dev(dx=1), dev(dx=3), dev(dy=1), dev(dy=3), dev(dz=1), dev(dz=3)
    SIB = dev(core=q)

    count = [0]
    sent = []

    def send(src, dst, device):
        i = count[0]
        count[0] += 1
        copy = pltpu.make_async_remote_copy(
            src_ref=src, dst_ref=dst, send_sem=send_sem.at[i], recv_sem=recv_sem.at[i],
            device_id=device, device_id_type=MESH)
        copy.start()
        sent.append(copy)
        return copy

    def arrive(copies):
        for copy in copies:
            copy.wait_recv()

    def left(copies):
        for copy in copies:
            copy.wait_send()
            sent[:] = [other for other in sent if other is not copy]

    loads = [
        pltpu.make_async_copy(src, dst, load_sem.at[i])
        for i, (src, dst) in enumerate(((f_hbm, f_raw), (w_hbm, w_raw), (cot_hbm, cot), (tiles_hbm, tiles)))
    ]
    for load in loads:
        load.start()
    load_f, load_w, load_cot, load_tiles = loads

    barrier = pltpu.get_barrier_semaphore()
    peers = [dev(dx=d) for d in (1, 2, 3)] + [dev(dy=d) for d in (1, 2, 3)] + [dev(dz=d) for d in (1, 2, 3)] + [SIB]
    for peer in peers:
        pl.semaphore_signal(barrier, inc=1, device_id=peer, device_id_type=MESH)

    F_IN = f_hbm.shape[0]
    tail = F_IN // 8 * 8
    ft_pad = gf_acc
    load_f.wait()
    ft_pad[pl.ds(tail, PAD - tail), :] = jnp.zeros((PAD - tail, ft_pad.shape[1]), F32)
    ft_pad[pl.ds(0, F_IN), :] = f_raw[...]
    f_hi[...], f_lo[...] = split(ft_pad[...].T)
    load_w.wait()
    w_pad[pl.ds(tail, PAD - tail), :] = jnp.zeros((PAD - tail, w_pad.shape[1]), F32)
    w_pad[pl.ds(0, F_IN), :] = w_raw[...]

    ag = [dict() for _ in range(C)]
    st = [dict() for _ in range(C)]

    def cols(h):
        return pl.ds(h * W, W)

    def project(h):
        out = mm((f_hi[...], f_lo[...]), split(w_pad[:, cols(h)]))
        G[h][x, y, p, 0] = out[:BLOCK]
        G[h][x, y, p, 1] = out[BLOCK:]

    def A1(h):
        own0, own1 = G[h].at[x, y, p, 0], G[h].at[x, y, p, 1]
        ag[h]["1"] = [send(own0, own0, XR), send(own0, own0, XL), send(own1, own1, YR), send(own1, own1, YL)]

    def A2(h):
        out = []
        for copy, ref, device in zip(
            ag[h]["1"],
            (G[h].at[xl, y, p, 0, LO], G[h].at[xr, y, p, 0, HI], G[h].at[x, yl, p, 1, LO], G[h].at[x, yr, p, 1, HI]),
            (XR, XL, YR, YL),
        ):
            copy.wait_recv()
            out.append(send(ref, ref, device))
        ag[h]["2"] = out

    def A3(h):
        arrive(ag[h]["2"])
        line0, line1 = G[h].at[:, y, p, 0], G[h].at[x, :, p, 1]
        ag[h]["3"] = [send(line0, line0, YR), send(line1, line1, XR), send(line0, line0, YL), send(line1, line1, XL)]
        ag[h]["5"] = [send(line0, line0, SIB), send(line1, line1, SIB)]

    def A4(h):
        out = []
        for copy, ref, device in zip(
            ag[h]["3"],
            (G[h].at[:, yl, p, 0, LO], G[h].at[xl, :, p, 1, LO], G[h].at[:, yr, p, 0, HI], G[h].at[xr, :, p, 1, HI]),
            (YR, XR, YL, XL),
        ):
            copy.wait_recv()
            out.append(send(ref, ref, device))
        ag[h]["4"] = out
        for line in (G[h].at[:, yl, p, 0], G[h].at[xl, :, p, 1], G[h].at[:, yr, p, 0], G[h].at[xr, :, p, 1]):
            ag[h]["5"].append(send(line, line, SIB))

    def A5(h):
        arrive(ag[h]["4"])
        for line in (G[h].at[:, yo, p, 0], G[h].at[xo, :, p, 1]):
            ag[h]["5"].append(send(line, line, SIB))

    def chain(base):
        def step(k, carry):
            slots[k] = slots[k] + slots[plan[base + k]]
            return carry
        lax.fori_loop(0, SLOTS, step, 0)

    def products(left_ref, load):
        def step(i, carry):
            out = []
            for j in range(4):
                k = i * 4 + j
                out.append(mm(split(left_ref[k]), split(load(k))))
            for j in range(4):
                slots[i * 4 + j] = out[j]
            return carry
        lax.fori_loop(0, SLOTS // 4, step, 0)

    def link_slots():
        lane = lax.broadcasted_iota(jnp.int32, (1, 128), 1)
        live = live_ref[0]
        for index, targets, prev, last in ((row_ref, ROWS, ROW_PREV, ROW_LAST), (col_ref, COLS, COL_PREV, COL_LAST)):
            held = jnp.full((1, 128), -1, jnp.int32)
            for k in range(SLOTS):
                held = jnp.where(lane == k, index[k], held)
            held = jnp.where(lane < live, held, -1)

            def find(match):
                best = jnp.max(jnp.where(match, lane, -1))
                return jnp.where(best < 0, SLOTS, best)

            def before(i, carry):
                for j in range(8):
                    k = i * 8 + j
                    plan[prev + k] = find((held == index[k]) & (lane < k))
                return carry
            lax.fori_loop(0, SLOTS // 8, before, 0)

            def final(i, carry):
                for j in range(8):
                    k = i * 8 + j
                    plan[last + k] = find(held == k)
                return carry
            lax.fori_loop(0, targets // 8, final, 0)

    def prepare():
        slots[SLOTS] = jnp.zeros(slots.shape[1:], F32)
        link_slots()
        load_tiles.wait()

        def turn(k, carry):
            tiles_t[k] = tiles[k].T
            return carry
        lax.fori_loop(0, SLOTS, turn, 0)
        ft_hi[...], ft_lo[...] = split(ft_pad[...])
        load_cot.wait()

    def F(h):
        arrive(ag[h]["5"])

        def load(k):
            c = col_ref[k]
            return G[h][c // 16, (c // 4) % 4, (c // 2) % 2, c % 2]
        products(tiles, load)
        chain(ROW_PREV)
        for i in range(2 * SIDE):
            part[h][i // 2, i % 2] = slots[plan[ROW_LAST + i]]

    def Z1(h):
        st[h]["z"] = [send(part[h].at[at(z, d)], zfin[h].at[d - 1], dev(dz=d)) for d in (1, 3, 2)]

    def Z3(h):
        arrive(st[h]["z"])
        for b in range(2):
            rows = pl.ds(b * BLOCK, BLOCK)
            s = (part[h][z, b] + zfin[h][0, b]) + (zfin[h][1, b] + zfin[h][2, b])
            sigma = jax.nn.sigmoid(s)
            act_ref[rows, cols(h)] = s * sigma
            GG[h][z, b] = cot[rows, cols(h)] * sigma * (1.0 + s * (1.0 - sigma))
        own = GG[h].at[z]
        st[h]["g"] = [send(own, own, dev(dz=d)) for d in (1, 3, 2)]

    def B(h):
        arrive(st[h]["g"])

        def load(k):
            c = row_ref[k]
            return GG[h][c // 2, c % 2]
        products(tiles_t, load)
        chain(COL_PREV)
        for copies in ag[h].values():
            left(copies)

        def place(core):
            def step(i, carry):
                for b in range(2):
                    G[h][i // 4, i % 4, core, b] = slots[plan[COL_LAST + i * 4 + core * 2 + b]]
                return carry
            lax.fori_loop(0, 16, step, 0)
        place(q)
        st[h]["sib"] = [send(G[h].at[:, :, q], R0[h], SIB)]
        place(p)

    def R1(h):
        arrive(st[h]["sib"])
        s, m, f = R0[h], m1[h], f1[h]

        def add(i, carry):
            s[i // 4, i % 4] = s[i // 4, i % 4] + G[h][i // 4, i % 4, p]
            return carry
        lax.fori_loop(0, 16, add, 0)
        st[h]["m1"] = [
            send(s.at[xo, :, 0, LO], m.at[0, 0], XR), send(s.at[:, yo, 1, LO], m.at[1, 0], YR),
            send(s.at[xo, :, 0, HI], m.at[0, 1], XL), send(s.at[:, yo, 1, HI], m.at[1, 1], YL)]
        st[h]["f1"] = [
            send(s.at[xr, :, 0, HI], f.at[0, 0, :, HI], XR), send(s.at[:, yr, 1, HI], f.at[1, 0, :, HI], YR),
            send(s.at[xl, :, 0, LO], f.at[0, 1, :, LO], XL), send(s.at[:, yl, 1, LO], f.at[1, 1, :, LO], YL)]

    def R2(h):
        s, m, f = R0[h], m1[h], f1[h]
        mid = st[h]["m1"]
        out = st[h]["f1"]
        mid[0].wait_recv()
        s[xr, :, 0, LO] = s[xr, :, 0, LO] + m[0, 0]
        out.append(send(s.at[xr, :, 0, LO], f.at[0, 0, :, LO], XR))
        mid[1].wait_recv()
        s[:, yr, 1, LO] = s[:, yr, 1, LO] + m[1, 0]
        out.append(send(s.at[:, yr, 1, LO], f.at[1, 0, :, LO], YR))
        mid[2].wait_recv()
        s[xl, :, 0, HI] = s[xl, :, 0, HI] + m[0, 1]
        out.append(send(s.at[xl, :, 0, HI], f.at[0, 1, :, HI], XL))
        mid[3].wait_recv()
        s[:, yl, 1, HI] = s[:, yl, 1, HI] + m[1, 1]
        out.append(send(s.at[:, yl, 1, HI], f.at[1, 1, :, HI], YL))

    def R3(h):
        arrive(st[h]["f1"])
        s, f = R0[h], f1[h]
        f[0, 0] = f[0, 0] + f[0, 1] + s[x, :, 0]
        f[1, 0] = f[1, 0] + f[1, 1] + s[:, y, 1]
        t0, t1, m, g = f.at[0, 0], f.at[1, 0], m2[h], f2[h]
        st[h]["m2"] = [
            send(t0.at[yo, LO], m.at[0, 0], YR), send(t1.at[xo, LO], m.at[1, 0], XR),
            send(t0.at[yo, HI], m.at[0, 1], YL), send(t1.at[xo, HI], m.at[1, 1], XL)]
        st[h]["f2"] = [
            send(t0.at[yr, HI], g.at[0, 0, HI], YR), send(t1.at[xr, HI], g.at[1, 0, HI], XR),
            send(t0.at[yl, LO], g.at[0, 1, LO], YL), send(t1.at[xl, LO], g.at[1, 1, LO], XL)]

    def R4(h):
        t, m, g = f1[h], m2[h], f2[h]
        mid = st[h]["m2"]
        out = st[h]["f2"]
        for copy, (b, i), rows, target, device in zip(
            mid, ((0, 0), (1, 0), (0, 1), (1, 1)), (LO, LO, HI, HI), (yr, xr, yl, xl), (YR, XR, YL, XL)
        ):
            copy.wait_recv()
            t[b, 0, target, rows] = t[b, 0, target, rows] + m[b, i]
            out.append(send(t.at[b, 0, target, rows], g.at[b, i, rows], device))

    def R5(h):
        arrive(st[h]["f2"])
        t, g = f1[h], f2[h]
        prop[pl.ds(0, BLOCK), cols(h)] = t[0, 0, y] + g[0, 0] + g[0, 1]
        prop[pl.ds(BLOCK, BLOCK), cols(h)] = t[1, 0, x] + g[1, 0] + g[1, 1]
        out = mm((ft_hi[...], ft_lo[...]), split(prop[:, cols(h)]))
        gwl[h][...] = out.reshape(2, SIDE, PAD // 8, W)
        st[h]["w1"] = [send(gwl[h].at[q], sb[h], SIB)]

    summed = []

    def grad_features(h):
        out = mm_nt(split(w_pad[:, cols(h)]), split(prop[:, cols(h)]))
        summed.append(h)
        if len(summed) == 1:
            gf_acc[...] = out
        else:
            gf_acc[...] = gf_acc[...] + out
        if len(summed) == C:
            gf_ref[...] = gf_acc[pl.ds(0, F_IN), :]

    def W2(h):
        arrive(st[h]["w1"])
        sb[h][...] = sb[h][...] + gwl[h][p]
        zb[h][z] = sb[h][z]
        st[h]["w2"] = [send(sb[h].at[at(z, d)], zb[h].at[z], dev(dz=d)) for d in (1, 2, 3)]

    def W3(h):
        arrive(st[h]["w2"])
        b = zb[h]
        xb[h][x] = (b[0] + b[1]) + (b[2] + b[3])
        own = xb[h].at[x]
        st[h]["w3"] = [send(own, own, dev(dx=d)) for d in (1, 2, 3)]

    def W4(h):
        arrive(st[h]["w3"])
        b = xb[h]
        yb[h][y] = (b[0] + b[1]) + (b[2] + b[3])
        own = yb[h].at[y]
        st[h]["w4"] = [send(own, own, dev(dy=d)) for d in (1, 2, 3)]

    def W5(h):
        arrive(st[h]["w4"])
        b = yb[h]
        gwo[h][p, z] = (b[0] + b[1]) + (b[2] + b[3])
        own = gwo[h].at[p, z]
        st[h]["w5"] = [send(own, own, dev(dz=d)) for d in (1, 2, 3)]

    def W6(h):
        arrive(st[h]["w5"])
        own = gwo[h].at[p]
        st[h]["w6"] = [send(own, own, SIB)]

    def W7(h):
        arrive(st[h]["w6"])
        gw_ref[:, cols(h)] = gwo[h][...].reshape(PAD, W)[:F_IN]

    stages = dict(P=project, A1=A1, A2=A2, A3=A3, A4=A4, A5=A5, F=F, Z1=Z1, Z3=Z3, B=B,
                  R1=R1, R2=R2, R3=R3, R4=R4, R5=R5, GF=grad_features, W2=W2, W3=W3, W4=W4, W5=W5, W6=W6, W7=W7)

    project(0)
    pl.semaphore_wait(barrier, len(peers))
    for name in " ".join(ORDER).split()[1:]:
        if name == "prep":
            prepare()
        else:
            stage, h = name.split("_")
            stages[stage](int(h))
    for copy in list(sent):
        copy.wait_send()


ORDER = (
    "P_0 A1_0 P_1 A1_1",
    "A2_0 P_2 A1_2 A2_1",
    "P_3 A3_0 A2_2 A1_3",
    "A4_0 A3_1 prep A5_0",
    "A3_2 F_0 Z1_0 A4_1",
    "A4_2 Z3_0 A2_3 A5_1",
    "F_1 Z1_1 A5_2 A3_3",
    "F_2 Z1_2 B_0 A4_3",
    "Z3_1 R1_0 A5_3 Z3_2",
    "F_3 R2_0 Z1_3 B_1",
    "R3_0 B_2 R4_0 R1_1",
    "Z3_3 R2_1 R1_2 B_3",
    "R3_1 R2_2 R5_0 R4_1",
    "R1_3 R2_3 W2_0 R5_1",
    "W2_1 R3_2 R3_3 R4_2",
    "R4_3 W3_1 R5_2 W3_0",
    "R5_3 W2_2 W2_3 W4_1",
    "GF_3 W3_2 GF_1 W4_0",
    "W5_1 W3_3 W4_2 W4_3",
    "W6_1 W5_0 W5_2 W5_3",
    "GF_2 W6_2 W6_0 W7_1",
    "W6_3 W7_2 W7_0 GF_0",
    "W7_3",
)


def body(features, weight, cotangent, tile_values, tile_row, tile_col, tile_count):
    hidden = weight.shape[1]
    nodes, width = features.shape
    C = CHUNKS
    W = hidden // C

    def vmem(*shape, dtype=F32, count=C):
        return [pltpu.VMEM(shape, dtype)] * count

    scratch = (
        vmem(4, 4, 2, 2, BLOCK, W)
        + vmem(4, 4, 2, BLOCK, W)
        + vmem(4, 2, BLOCK, W)
        + vmem(3, 2, BLOCK, W)
        + vmem(4, 2, BLOCK, W)
        + vmem(2, 2, 4, HALF, W)
        + vmem(2, 2, 4, BLOCK, W)
        + vmem(2, 2, HALF, W)
        + vmem(2, 2, BLOCK, W)
        + vmem(2, 4, PAD // 8, W)
        + vmem(4, PAD // 8, W)
        + vmem(4, PAD // 8, W)
        + vmem(4, PAD // 8, W)
        + vmem(4, PAD // 8, W)
        + vmem(2, 4, PAD // 8, W)
        + [
            pltpu.VMEM((SLOTS + 1, BLOCK, W), F32),
            pltpu.VMEM((SLOTS, BLOCK, BLOCK), F32),
            pltpu.VMEM((SLOTS, BLOCK, BLOCK), F32),
            pltpu.VMEM((width, hidden), F32),
            pltpu.VMEM((PAD, hidden), F32),
            pltpu.VMEM((width, nodes), F32),
            pltpu.VMEM((nodes, hidden), F32),
            pltpu.VMEM((nodes, PAD), BF16),
            pltpu.VMEM((nodes, PAD), BF16),
            pltpu.VMEM((PAD, nodes), BF16),
            pltpu.VMEM((PAD, nodes), BF16),
            pltpu.VMEM((nodes, hidden), F32),
            pltpu.VMEM((PAD, nodes), F32),
            pltpu.SMEM((2 * SLOTS + ROWS + COLS,), jnp.int32),
            pltpu.SemaphoreType.DMA((COPIES,)),
            pltpu.SemaphoreType.DMA((COPIES,)),
            pltpu.SemaphoreType.DMA((4,)),
        ]
    )
    whole = pl.BlockSpec(memory_space=pltpu.VMEM)
    scalars = pl.BlockSpec(memory_space=pltpu.SMEM)
    hbm = pl.BlockSpec(memory_space=pl.ANY)
    activated, grad_features, grad_weight = pl.pallas_call(
        kernel,
        out_shape=(
            jax.ShapeDtypeStruct((nodes, hidden), F32),
            jax.ShapeDtypeStruct((width, nodes), F32),
            jax.ShapeDtypeStruct((width, hidden), F32),
        ),
        in_specs=[scalars] * 3 + [hbm] * 4,
        out_specs=(whole, whole, whole),
        scratch_shapes=scratch,
        compiler_params=pltpu.CompilerParams(
            collective_id=0, has_side_effects=True, vmem_limit_bytes=62 * 1024 * 1024),
    )(tile_row, tile_col, tile_count, features.T, weight, cotangent, tile_values)
    return activated, grad_features.T, grad_weight


def solution(mesh):
    in_specs = (
        P(("rows", "rep"), None),
        P(),
        P(("rows", "rep"), None),
        P(("rows", "rep"), None, None),
        P(("rows", "rep")),
        P(("rows", "rep")),
        P(("rows", "rep")),
    )
    out_specs = (P(("rows", "rep"), None), P(("rows", "rep"), None), P())
    return jax.shard_map(body, mesh=mesh, in_specs=in_specs, out_specs=out_specs, check_vma=False)
```

time: 597 us -> 150 us (0.25)
  waiting for transfers between devices: 419 us -> 0 us
  Pallas kernels: 0 us -> 144 us
  local copies, waits for them, and re-layouts: 82.2 us -> 4.95 us
  matrix products: 40.3 us -> 0 us
  other arithmetic: 40.2 us -> 0 us
  between operations: 14.5 us -> 1.3 us
    psum x1 -> x0, waiting for transfers between devices: 147 us -> none  [body(): grad_weight = lax.psum(local_weight, ('rows', 'rep'))]
    reduce_scatter x2 -> x0, waiting for transfers between devices: 147 us -> none  [the longest x1 113 us: body(): lax.psum_scatter(column_part, 'rows', scatter_dimension=0, tiled=True)]
    pallas_call x0 -> x1, Pallas kernels: none -> 144 us  [body(): pl.pallas_call(kernel, out_shape=(jax.ShapeDtypeStruct((nodes, hidden), F...]
    all_gather x2 -> x0, waiting for transfers between devices: 124 us -> none  [the longest x1 93.1 us: body(): gathered = lax.all_gather(features, 'rows', axis=0, tiled=True)]
    dot_general x5 -> x0, matrix products: 40.3 us -> none  [the longest x2 29.9 us: slot_term(): product = jnp.einsum(pattern, values, picked, precision=highest)]
    scatter-add x2 -> x0, other arithmetic: 38.8 us -> none  [slot_term(): return empty.at[put_index].add(product)]
    reshape x2 -> x0, local copies, waits for them, and re-layouts: 27.6 us -> none  [body(): gathered.reshape(columns, BLOCK, -1)]
    gather x2 -> x0, local copies, waits for them, and re-layouts: 17.5 us -> none  [slot_term(): picked = source[take_index]]
  transfers between devices with their start and end apart: 5 -> 0, of which waited for: 5 -> 0; matrix products, arithmetic and copies ran while one was open for 1% -> 0% of each run, Pallas kernels for 0% -> 0%
where the time goes in v1:
time: 150 us
  Pallas kernels  144 us (96%)
  local copies, waits for them, and re-layouts  4.95 us (3%)
    pallas_call x1, Pallas kernels, body(): pl.pallas_call(kernel, out_shape=(jax.ShapeDtypeStruct((nodes, hidden), F...  144 us
    unnamed x5, local copies, waits for them, and re-layouts  4.95 us

profile of v1, /device:TPU:1, one launch (start us, length us, event | category | flops | bytes accessed | tf_op | source)
XLA Modules:
  0.0 149.9 jit_solution(11991131388102797025)
XLA Ops:
  1.3 143.6 %shard_map.94 = (f32[256,512]{1,0:T(8,128)}, f32[602,256]{1,0:T(8,128)}, f32[602,512]{1,0:T(8,128)}) custom-call(s32[32]{0:T(128)} %refs_0_.1, s32[32]{0:T(128)} %refs_1_.1, s32[1]{0:T(128)S(6)} %copy.13.refs_2_, f32[602,256]{1,0:T(8,128)} %bitcast.3, f32[602,512]{1,0:T(8,128)} %refs_4_.1, f32[256,512]{1,0:T(8,128)} %refs_5_.1, f32[32,128,128]{2,1,0:T(8,128)} %refs_6_.1), custom_call_target="tpu_custom_call" | custom-call | tf_op jit(solution)/shard_map/pallas_call | solution.py:481
  144.9 0.0 copy-start
  144.9 2.0 %copy.14 = f32[256,512]{1,0:T(8,128)} copy(f32[256,512]{1,0:T(8,128)} %get-tuple-element.12) | data formatting | bytes 1048576
  146.9 1.9 %copy.15 = f32[256,602]{0,1:T(8,128)} copy(f32[256,602]{0,1:T(8,128)} %bitcast.2) | data formatting | bytes 1232896
  148.8 0.0 copy-done
  148.8 1.0 copy.16
Async XLA Ops:
  144.9 3.9 %copy-start = (f32[602,512]{1,0:T(8,128)S(1)}, f32[602,512]{1,0:T(8,128)}, u32[]{:S(2)}) copy-start(f32[602,512]{1,0:T(8,128)} %get-tuple-element.14) | copy-start | bytes 3698692

commit v2 on v1

v2 whole, which is shorter than its diff:
```python
import functools
import math

import jax
import jax.numpy as jnp
from jax import lax
from jax.experimental import pallas as pl
from jax.experimental.pallas import tpu as pltpu
from jax.sharding import PartitionSpec as P

MESH = pl.DeviceIdType.MESH
F32 = jnp.float32
BF16 = jnp.bfloat16

BLOCK = 128
HALF = BLOCK // 2
SLOTS = 32
CHUNKS = 4
SIDE = 4
PAD = 640
GROUPS = 19

ROWS, COLS = 8, 64
ROW_PREV, ROW_LAST, COL_PREV, COL_LAST = 0, SLOTS, SLOTS + ROWS, 2 * SLOTS + ROWS

LO, HI = pl.ds(0, HALF), pl.ds(HALF, HALF)
GATHER = ("a1", "a2", "a3", "a4", "a5")


def split(value):
    high = value.astype(BF16)
    return high, (value - high.astype(F32)).astype(BF16)


def mm(a, b):
    left = jnp.concatenate([a[0], a[1], a[0]], axis=1)
    right = jnp.concatenate([b[0], b[0], b[1]], axis=0)
    return jnp.dot(left, right, preferred_element_type=F32)


def mm_nt(a, b):
    left = jnp.concatenate([a[0], a[1], a[0]], axis=1)
    right = jnp.concatenate([b[0], b[0], b[1]], axis=1)
    return lax.dot_general(left, right, (((1,), (1,)), ((), ())), preferred_element_type=F32)


def kernel(*refs):
    C = CHUNKS
    row_ref, col_ref, live_ref, f_hbm, w_hbm, cot_hbm, tiles_hbm, act_hbm, gf_hbm, gw_hbm = refs[:10]
    refs = list(refs[10:])

    def take(count):
        out = refs[:count]
        del refs[:count]
        return out

    G, R0, part, zmid, zfin, GG = (take(C) for _ in range(6))
    m1, f1, m2, f2 = (take(C) for _ in range(4))
    gwl, sb, wa, wb, wc, gwo = (take(C) for _ in range(6))
    slots, tiles, tiles_t, w_raw, w_pad, f_raw, cot, f_hi, f_lo, ft_hi, ft_lo, prop, gf_acc, plan = take(14)
    act, gf, gw = take(3)
    send_sem, recv_sem, load_sem, store_sem = take(4)
    W = prop.shape[1] // C

    r = lax.axis_index("rows")
    z = lax.axis_index("rep")
    x, y, p = r // 8, (r // 2) % 4, r % 2
    q = 1 - p

    def at(i, d):
        return (i + d) % SIDE

    def dev(dx=0, dy=0, dz=0, core=None):
        c = p if core is None else core
        return (at(x, dx) * 8 + at(y, dy) * 2 + c, at(z, dz))

    xl, xr, xo = at(x, 3), at(x, 1), at(x, 2)
    yl, yr, yo = at(y, 3), at(y, 1), at(y, 2)
    zl, zr, zo = at(z, 3), at(z, 1), at(z, 2)
    XR, XL, YR, YL, ZR, ZL = dev(dx=1), dev(dx=3), dev(dy=1), dev(dy=3), dev(dz=1), dev(dz=3)
    SIB = dev(core=q)

    stores = []

    def store(src, dst):
        copy = pltpu.make_async_copy(src, dst, store_sem.at[len(stores)])
        copy.start()
        stores.append(copy)

    ready = []

    def need(load):
        if not any(load is other for other in ready):
            load.wait()
            ready.append(load)

    names = [[] for _ in range(C)]
    lines = {}
    leaving = []

    def spot(group):
        chunk, name = group
        if name not in names[chunk]:
            names[chunk].append(name)
        return GROUPS * chunk + names[chunk].index(name)

    def send(src, dst, device, group):
        copy = pltpu.make_async_remote_copy(
            src_ref=src, dst_ref=dst, send_sem=send_sem.at[spot(group)], recv_sem=recv_sem.at[spot(group)],
            device_id=device, device_id_type=MESH)
        copy.start()
        if group not in lines:
            lines[group] = 0
            leaving.append(group)
        lines[group] += math.prod(src.shape) // W

    def all_of(group):
        count = lines[group]
        ref = slots.at[pl.ds(0, count // BLOCK)] if count % BLOCK == 0 else sb[0].at[pl.ds(0, count)]
        return pltpu.make_async_remote_copy(
            src_ref=ref, dst_ref=ref, send_sem=send_sem.at[spot(group)], recv_sem=recv_sem.at[spot(group)],
            device_id=XR, device_id_type=MESH)

    def arrive(*group):
        all_of(group).wait_recv()

    def left(h, *which):
        for name in which:
            all_of((h, name)).wait_send()
            leaving.remove((h, name))

    def drain():
        for group in list(leaving):
            left(*group)

    loads = [
        pltpu.make_async_copy(src, dst, load_sem.at[i])
        for i, (src, dst) in enumerate(((f_hbm, f_raw), (w_hbm, w_raw), (cot_hbm, cot), (tiles_hbm, tiles)))
    ]
    load_f, load_w, load_cot, load_tiles = loads
    load_f.start()
    load_w.start()

    barrier = pltpu.get_barrier_semaphore()
    peers = [dev(dx=d) for d in (1, 2, 3)] + [dev(dy=d) for d in (1, 2, 3)] + [dev(dz=d) for d in (1, 2, 3)] + [SIB]
    for peer in peers:
        pl.semaphore_signal(barrier, inc=1, device_id=peer, device_id_type=MESH)

    F_IN = f_hbm.shape[0]
    tail = F_IN // 8 * 8
    ft_pad = gf_acc
    load_f.wait()
    ft_pad[pl.ds(tail, PAD - tail), :] = jnp.zeros((PAD - tail, ft_pad.shape[1]), F32)
    ft_pad[pl.ds(0, F_IN), :] = f_raw[...]
    f_hi[...], f_lo[...] = split(ft_pad[...].T)
    load_w.wait()
    w_pad[pl.ds(tail, PAD - tail), :] = jnp.zeros((PAD - tail, w_pad.shape[1]), F32)
    w_pad[pl.ds(0, F_IN), :] = w_raw[...]

    def cols(h):
        return pl.ds(h * W, W)

    def project(h):
        out = mm((f_hi[...], f_lo[...]), split(w_pad[:, cols(h)]))
        G[h][x, y, p, 0] = out[:BLOCK]
        G[h][x, y, p, 1] = out[BLOCK:]

    def A1(h):
        own0, own1 = G[h].at[x, y, p, 0], G[h].at[x, y, p, 1]
        g = (h, "a1")
        for ref, device in ((own0, XR), (own0, XL), (own1, YR), (own1, YL)):
            send(ref, ref, device, g)

    def A2(h):
        arrive(h, "a1")
        for ref, device in (
            (G[h].at[xl, y, p, 0, LO], XR), (G[h].at[xr, y, p, 0, HI], XL),
            (G[h].at[x, yl, p, 1, LO], YR), (G[h].at[x, yr, p, 1, HI], YL),
        ):
            send(ref, ref, device, (h, "a2"))

    def A3(h):
        arrive(h, "a2")
        line0, line1 = G[h].at[:, y, p, 0], G[h].at[x, :, p, 1]
        for line, device in ((line0, YR), (line1, XR), (line0, YL), (line1, XL)):
            send(line, line, device, (h, "a3"))
        for line in (line0, line1):
            send(line, line, SIB, (h, "a5"))

    def A4(h):
        arrive(h, "a3")
        for ref, device in (
            (G[h].at[:, yl, p, 0, LO], YR), (G[h].at[xl, :, p, 1, LO], XR),
            (G[h].at[:, yr, p, 0, HI], YL), (G[h].at[xr, :, p, 1, HI], XL),
        ):
            send(ref, ref, device, (h, "a4"))
        for line in (G[h].at[:, yl, p, 0], G[h].at[xl, :, p, 1], G[h].at[:, yr, p, 0], G[h].at[xr, :, p, 1]):
            send(line, line, SIB, (h, "a5"))

    def A5(h):
        arrive(h, "a4")
        for line in (G[h].at[:, yo, p, 0], G[h].at[xo, :, p, 1]):
            send(line, line, SIB, (h, "a5"))

    def chain(base):
        def step(k, carry):
            slots[k] = slots[k] + slots[plan[base + k]]
            return carry
        lax.fori_loop(0, SLOTS, step, 0)

    def products(left_ref, load):
        def step(i, carry):
            out = []
            for j in range(4):
                k = i * 4 + j
                out.append(mm(split(left_ref[k]), split(load(k))))
            for j in range(4):
                slots[i * 4 + j] = out[j]
            return carry
        lax.fori_loop(0, SLOTS // 4, step, 0)

    def link_slots():
        lane = lax.broadcasted_iota(jnp.int32, (1, 128), 1)
        live = live_ref[0]
        for index, targets, prev, last in ((row_ref, ROWS, ROW_PREV, ROW_LAST), (col_ref, COLS, COL_PREV, COL_LAST)):
            held = jnp.full((1, 128), -1, jnp.int32)
            for k in range(SLOTS):
                held = jnp.where(lane == k, index[k], held)
            held = jnp.where(lane < live, held, -1)

            def find(match):
                best = jnp.max(jnp.where(match, lane, -1))
                return jnp.where(best < 0, SLOTS, best)

            def before(i, carry):
                for j in range(8):
                    k = i * 8 + j
                    plan[prev + k] = find((held == index[k]) & (lane < k))
                return carry
            lax.fori_loop(0, SLOTS // 8, before, 0)

            def final(i, carry):
                for j in range(8):
                    k = i * 8 + j
                    plan[last + k] = find(held == k)
                return carry
            lax.fori_loop(0, targets // 8, final, 0)

    def link():
        slots[SLOTS] = jnp.zeros(slots.shape[1:], F32)
        link_slots()

    def turn_tiles():
        def turn(k, carry):
            tiles_t[k] = tiles[k].T
            return carry
        need(load_tiles)
        lax.fori_loop(0, SLOTS, turn, 0)

    def split_features():
        ft_hi[...], ft_lo[...] = split(ft_pad[...])

    def F(h):
        need(load_tiles)
        arrive(h, "a5")

        def load(k):
            c = col_ref[k]
            return G[h][c // 16, (c // 4) % 4, (c // 2) % 2, c % 2]
        products(tiles, load)
        chain(ROW_PREV)
        for i in range(2 * SIDE):
            part[h][i // 2, i % 2] = slots[plan[ROW_LAST + i]]

    def Z1(h):
        a, b = part[h], zfin[h]
        send(a.at[zo, 0], zmid[h].at[0], ZR, (h, "z1"))
        send(a.at[zo, 1], zmid[h].at[1], ZL, (h, "z1"))
        send(a.at[zr, 1], b.at[0, 1], ZR, (h, "z2"))
        send(a.at[zl, 0], b.at[1, 0], ZL, (h, "z2"))

    def Z2(h):
        a, b = part[h], zfin[h]
        arrive(h, "z1")
        a[zr, 0] = a[zr, 0] + zmid[h][0]
        send(a.at[zr, 0], b.at[0, 0], ZR, (h, "z2"))
        a[zl, 1] = a[zl, 1] + zmid[h][1]
        send(a.at[zl, 1], b.at[1, 1], ZL, (h, "z2"))

    def Z3(h):
        arrive(h, "z2")
        need(load_cot)
        for b in range(2):
            rows = pl.ds(b * BLOCK, BLOCK)
            s = part[h][z, b] + zfin[h][0, b] + zfin[h][1, b]
            sigma = jax.nn.sigmoid(s)
            act[rows, cols(h)] = s * sigma
            GG[h][z, b] = cot[rows, cols(h)] * sigma * (1.0 + s * (1.0 - sigma))
        store(act.at[:, cols(h)], act_hbm.at[:, cols(h)])
        own = GG[h].at[z]
        for d in (1, 3, 2):
            send(own, own, dev(dz=d), (h, "g"))

    def B(h):
        arrive(h, "g")

        def load(k):
            c = row_ref[k]
            return GG[h][c // 2, c % 2]
        products(tiles_t, load)
        chain(COL_PREV)
        left(h, *GATHER)

        def place(core, b):
            def step(i, carry):
                for j in range(2):
                    k = i * 2 + j
                    G[h][k // 4, k % 4, core, b] = slots[plan[COL_LAST + k * 4 + core * 2 + b]]
                return carry
            lax.fori_loop(0, 8, step, 0)
        for b in range(2):
            place(q, b)
            send(G[h].at[:, :, q, b], R0[h].at[:, :, b], SIB, (h, "s" + str(b)))
        for b in range(2):
            place(p, b)

    def with_own(h, b):
        arrive(h, "s" + str(b))
        s = R0[h]

        def add(i, carry):
            s[i // 4, i % 4, b] = s[i // 4, i % 4, b] + G[h][i // 4, i % 4, p, b]
            return carry
        lax.fori_loop(0, 16, add, 0)

    def R1a(h):
        with_own(h, 0)
        s, m, f = R0[h], m1[h], f1[h]
        send(s.at[xo, :, 0, LO], m.at[0, 0], XR, (h, "m1"))
        send(s.at[xo, :, 0, HI], m.at[0, 1], XL, (h, "m1"))
        send(s.at[xr, :, 0, HI], f.at[0, 0, :, HI], XR, (h, "f1"))
        send(s.at[xl, :, 0, LO], f.at[0, 1, :, LO], XL, (h, "f1"))

    def R1b(h):
        with_own(h, 1)
        s, m, f = R0[h], m1[h], f1[h]
        send(s.at[:, yo, 1, LO], m.at[1, 0], YR, (h, "m1"))
        send(s.at[:, yo, 1, HI], m.at[1, 1], YL, (h, "m1"))
        send(s.at[:, yr, 1, HI], f.at[1, 0, :, HI], YR, (h, "f1"))
        send(s.at[:, yl, 1, LO], f.at[1, 1, :, LO], YL, (h, "f1"))

    def R2(h):
        s, m, f = R0[h], m1[h], f1[h]
        g = (h, "f1")
        arrive(h, "m1")
        s[xr, :, 0, LO] = s[xr, :, 0, LO] + m[0, 0]
        send(s.at[xr, :, 0, LO], f.at[0, 0, :, LO], XR, g)
        s[:, yr, 1, LO] = s[:, yr, 1, LO] + m[1, 0]
        send(s.at[:, yr, 1, LO], f.at[1, 0, :, LO], YR, g)
        s[xl, :, 0, HI] = s[xl, :, 0, HI] + m[0, 1]
        send(s.at[xl, :, 0, HI], f.at[0, 1, :, HI], XL, g)
        s[:, yl, 1, HI] = s[:, yl, 1, HI] + m[1, 1]
        send(s.at[:, yl, 1, HI], f.at[1, 1, :, HI], YL, g)

    def R3(h):
        arrive(h, "f1")
        s, f = R0[h], f1[h]
        f[0, 0] = f[0, 0] + f[0, 1] + s[x, :, 0]
        f[1, 0] = f[1, 0] + f[1, 1] + s[:, y, 1]
        t0, t1, m, b = f.at[0, 0], f.at[1, 0], m2[h], f2[h]
        g = (h, "f2")
        if h == C - 1:
            send(t0.at[yr], b.at[0, 0], YR, g)
            send(t1.at[xr], b.at[1, 0], XR, g)
            send(t0.at[yl], b.at[0, 1], YL, g)
            send(t1.at[xl], b.at[1, 1], XL, g)
            send(t0.at[yo], m.at[0], dev(dy=2), g)
            send(t1.at[xo], m.at[1], dev(dx=2), g)
            return
        send(t0.at[yo, LO], m.at[0, 0], YR, (h, "m2"))
        send(t1.at[xo, LO], m.at[1, 0], XR, (h, "m2"))
        send(t0.at[yo, HI], m.at[0, 1], YL, (h, "m2"))
        send(t1.at[xo, HI], m.at[1, 1], XL, (h, "m2"))
        send(t0.at[yr, HI], b.at[0, 0, HI], YR, g)
        send(t1.at[xr, HI], b.at[1, 0, HI], XR, g)
        send(t0.at[yl, LO], b.at[0, 1, LO], YL, g)
        send(t1.at[xl, LO], b.at[1, 1, LO], XL, g)

    def R4(h):
        if h == C - 1:
            return
        t, m, b = f1[h], m2[h], f2[h]
        arrive(h, "m2")
        for (i, j), rows, target, device in zip(
            ((0, 0), (1, 0), (0, 1), (1, 1)), (LO, LO, HI, HI), (yr, xr, yl, xl), (YR, XR, YL, XL)
        ):
            t[i, 0, target, rows] = t[i, 0, target, rows] + m[i, j]
            send(t.at[i, 0, target, rows], b.at[i, j, rows], device, (h, "f2"))

    def R5(h):
        arrive(h, "f2")
        t, g = f1[h], f2[h]
        own0, own1 = t[0, 0, y] + g[0, 0] + g[0, 1], t[1, 0, x] + g[1, 0] + g[1, 1]
        if h == C - 1:
            own0, own1 = own0 + m2[h][0], own1 + m2[h][1]
        prop[pl.ds(0, BLOCK), cols(h)] = own0
        prop[pl.ds(BLOCK, BLOCK), cols(h)] = own1
        right = split(prop[:, cols(h)])

        def weight_half(core):
            rows = pl.ds(pl.multiple_of(core * (PAD // 2), PAD // 2), PAD // 2)
            gwl[h][core] = mm((ft_hi[rows, :], ft_lo[rows, :]), right)
        weight_half(q)
        send(gwl[h].at[q], sb[h], SIB, (h, "w1"))
        weight_half(p)

    summed = []

    def grad_features(h):
        out = mm_nt(split(w_pad[:, cols(h)]), split(prop[:, cols(h)]))
        summed.append(h)
        if len(summed) == 1:
            gf_acc[...] = out
        else:
            gf_acc[...] = gf_acc[...] + out
        if len(summed) == C:
            gf[...] = gf_acc[pl.ds(0, F_IN), :]
            store(gf, gf_hbm)

    me = dict(x=x, y=y, z=z)

    def peers_of(axis):
        return [(at(me[axis], d), dev(**{"d" + axis: d})) for d in (1, 3, 2)]

    def groups(h):
        if h < C - 1:
            return [(0, PAD // 8, pl.ds(0, PAD // 8), "zxyz")]
        n = PAD // 16
        return [(0, n, pl.ds(0, n), "zxyz"), (4 * n, n, pl.ds(n, n), "yzxy")]

    def piece(first, n, i):
        return pl.ds(pl.multiple_of(first + i * n, 8), n)

    def total(b, part_of):
        return (b[0, part_of] + b[1, part_of]) + (b[2, part_of] + b[3, part_of])

    def W2(h):
        arrive(h, "w1")
        sb[h][...] = sb[h][...] + gwl[h][p]
        for first, n, spot, axes in groups(h):
            mine = me[axes[0]]
            wa[h][mine, spot] = sb[h][piece(first, n, mine)]
            for i, device in peers_of(axes[0]):
                send(sb[h].at[piece(first, n, i)], wa[h].at[mine, spot], device, (h, "w2"))

    def exchange(h, before, after, source, target, step):
        arrive(h, before)
        for first, n, spot, axes in groups(h):
            mine = me[axes[step]]
            target[mine, spot] = total(source, spot)
            own = target.at[mine, spot]
            for i, device in peers_of(axes[step]):
                send(own, own, device, (h, after))

    def W3(h):
        exchange(h, "w2", "w3", wa[h], wb[h], 1)

    def W4(h):
        exchange(h, "w3", "w4", wb[h], wc[h], 2)

    def W5(h):
        arrive(h, "w4")
        for first, n, spot, axes in groups(h):
            rows = piece(first, n, me[axes[3]])
            gwo[h][p, rows] = total(wc[h], spot)
            own = gwo[h].at[p, rows]
            for i, device in peers_of(axes[3]):
                send(own, own, device, (h, "w5"))

    def W6(h):
        arrive(h, "w5")
        own = gwo[h].at[p]
        send(own, own, SIB, (h, "w6"))

    def W7(h):
        arrive(h, "w6")
        half = PAD // 2
        gw[pl.ds(0, half), cols(h)] = gwo[h][0]
        gw[pl.ds(half, F_IN - half), cols(h)] = gwo[h][1, pl.ds(0, F_IN - half)]
        store(gw.at[:, cols(h)], gw_hbm.at[:, cols(h)])

    stages = dict(P=project, A1=A1, A2=A2, A3=A3, A4=A4, A5=A5, F=F, Z1=Z1, Z2=Z2, Z3=Z3, B=B,
                  R1a=R1a, R1b=R1b, R2=R2, R3=R3, R4=R4, R5=R5, GF=grad_features, W2=W2, W3=W3, W4=W4, W5=W5, W6=W6, W7=W7)

    alone = dict(plan=link, turn=turn_tiles, ft=split_features, drain=drain)
    project(0)
    load_tiles.start()
    load_cot.start()
    pl.semaphore_wait(barrier, len(peers))
    for name in " ".join(ORDER).split()[1:]:
        if name in alone:
            alone[name]()
        else:
            stage, h = name.split("_")
            stages[stage](int(h))
    drain()
    for copy in stores:
        copy.wait()


ORDER = (
    "P_0 P_1 A1_1 P_2",
    "P_3 A1_0 A2_1 A1_2",
    "A1_3 ft A3_1 A2_0",
    "turn A2_2 plan A2_3",
    "A4_1 A3_0 A3_2 A5_1",
    "F_1 Z1_1 Z2_1 A4_0",
    "A4_2 A3_3 Z3_1 A5_0",
    "A5_2 F_0 Z1_0 F_2",
    "Z1_2 B_1 Z2_0 A4_3",
    "Z2_2 R1a_1 Z3_0 R1b_1",
    "Z3_2 A5_3 F_3 Z1_3",
    "R2_1 B_0 R3_1 R1a_0",
    "Z2_3 R4_1 R1b_0 B_2",
    "Z3_3 R2_0 R1b_2 R1a_2",
    "R5_1 GF_1 R3_0 B_3",
    "R2_2 R4_0 R1a_3 W2_1",
    "R1b_3 R5_0 R3_2 GF_0",
    "R2_3 W2_0 R4_2 W3_1",
    "R3_3 R5_2 W4_1 GF_2",
    "W2_2 W3_0 R4_3 R5_3",
    "GF_3 W3_2 W2_3 W4_0",
    "W5_1 W3_3 W4_2 W6_1",
    "W5_0 drain W4_3 W5_2",
    "W6_0 W5_3 W7_0 W6_2",
    "W7_1 W6_3 W7_2 W7_3",
)


def hand_over(*refs):
    copies = [pltpu.make_async_copy(refs[i], refs[3 + i], refs[6].at[i]) for i in range(3)]
    for copy in copies:
        copy.start()
    for copy in copies:
        copy.wait()


def body(features, weight, cotangent, tile_values, tile_row, tile_col, tile_count):
    hidden = weight.shape[1]
    nodes, width = features.shape
    C = CHUNKS
    W = hidden // C

    def vmem(*shape, dtype=F32, count=C):
        return [pltpu.VMEM(shape, dtype)] * count

    scratch = (
        vmem(4, 4, 2, 2, BLOCK, W)
        + vmem(4, 4, 2, BLOCK, W)
        + vmem(4, 2, BLOCK, W)
        + vmem(2, BLOCK, W)
        + vmem(2, 2, BLOCK, W)
        + vmem(4, 2, BLOCK, W)
        + vmem(2, 2, 4, HALF, W)
        + vmem(2, 2, 4, BLOCK, W)
        + vmem(2, 2, HALF, W, count=C - 1)
        + vmem(2, BLOCK, W, count=1)
        + vmem(2, 2, BLOCK, W)
        + vmem(2, PAD // 2, W)
        + vmem(PAD // 2, W)
        + vmem(4, PAD // 8, W)
        + vmem(4, PAD // 8, W)
        + vmem(4, PAD // 8, W)
        + vmem(2, PAD // 2, W)
        + [
            pltpu.VMEM((SLOTS + 1, BLOCK, W), F32),
            pltpu.VMEM((SLOTS, BLOCK, BLOCK), F32),
            pltpu.VMEM((SLOTS, BLOCK, BLOCK), F32),
            pltpu.VMEM((width, hidden), F32),
            pltpu.VMEM((PAD, hidden), F32),
            pltpu.VMEM((width, nodes), F32),
            pltpu.VMEM((nodes, hidden), F32),
            pltpu.VMEM((nodes, PAD), BF16),
            pltpu.VMEM((nodes, PAD), BF16),
            pltpu.VMEM((PAD, nodes), BF16),
            pltpu.VMEM((PAD, nodes), BF16),
            pltpu.VMEM((nodes, hidden), F32),
            pltpu.VMEM((PAD, nodes), F32),
            pltpu.SMEM((2 * SLOTS + ROWS + COLS,), jnp.int32),
            pltpu.VMEM((nodes, hidden), F32),
            pltpu.VMEM((width, nodes), F32),
            pltpu.VMEM((width, hidden), F32),
            pltpu.SemaphoreType.DMA((GROUPS * C,)),
            pltpu.SemaphoreType.DMA((GROUPS * C,)),
            pltpu.SemaphoreType.DMA((4,)),
            pltpu.SemaphoreType.DMA((2 * C + 1,)),
        ]
    )
    scalars = pl.BlockSpec(memory_space=pltpu.SMEM)
    hbm = pl.BlockSpec(memory_space=pl.ANY)
    shapes = (
        jax.ShapeDtypeStruct((nodes, hidden), F32),
        jax.ShapeDtypeStruct((width, nodes), F32),
        jax.ShapeDtypeStruct((width, hidden), F32),
    )
    results = pl.pallas_call(
        kernel,
        out_shape=shapes,
        in_specs=[scalars] * 3 + [hbm] * 4,
        out_specs=(hbm, hbm, hbm),
        scratch_shapes=scratch,
        compiler_params=pltpu.CompilerParams(
            collective_id=0, has_side_effects=True, vmem_limit_bytes=62 * 1024 * 1024),
    )(tile_row, tile_col, tile_count, features.T, weight, cotangent, tile_values)
    activated, grad_features, grad_weight = pl.pallas_call(
        hand_over,
        out_shape=shapes,
        in_specs=[pl.BlockSpec(memory_space=pltpu.VMEM)] * 3,
        out_specs=(hbm,) * 3,
        scratch_shapes=[pltpu.SemaphoreType.DMA((3,))],
    )(*results)
    return activated, grad_features.T, grad_weight


def solution(mesh):
    in_specs = (
        P(("rows", "rep"), None),
        P(),
        P(("rows", "rep"), None),
        P(("rows", "rep"), None, None),
        P(("rows", "rep")),
        P(("rows", "rep")),
        P(("rows", "rep")),
    )
    out_specs = (P(("rows", "rep"), None), P(("rows", "rep"), None), P())
    return jax.shard_map(body, mesh=mesh, in_specs=in_specs, out_specs=out_specs, check_vma=False)
```

time: 150 us -> 139 us (0.927)
  Pallas kernels: 144 us -> 138 us
  local copies, waits for them, and re-layouts: 4.95 us -> 0 us
    pallas_call x1 -> x2, Pallas kernels: 144 us -> 138 us  [the longest x1 135 us: body(): pl.pallas_call(kernel, out_shape=shapes, in_specs=[scalars] * 3 + [hbm] *...]
    unnamed x5 -> x0, local copies, waits for them, and re-layouts: 4.95 us -> none
where the time goes in v2:
time: 139 us
  Pallas kernels  138 us (99%)
    pallas_call x1, Pallas kernels, body(): pl.pallas_call(kernel, out_shape=shapes, in_specs=[scalars] * 3 + [hbm] *...  135 us
    pallas_call x1, Pallas kernels, body(): pl.pallas_call(hand_over, out_shape=shapes, in_specs=[pl.BlockSpec(memory...  3.08 us

profile of v2, /device:TPU:1, one launch (start us, length us, event | category | flops | bytes accessed | tf_op | source)
XLA Modules:
  0.0 139.0 jit_solution(15218506831669541896)
XLA Ops:
  1.3 134.6 %shard_map.94 = (f32[256,512]{1,0:T(8,128)}, f32[602,256]{1,0:T(8,128)}, f32[602,512]{1,0:T(8,128)}) custom-call(s32[32]{0:T(128)} %refs_0_.1, s32[32]{0:T(128)} %refs_1_.1, s32[1]{0:T(128)S(6)} %copy.10.refs_2_, f32[602,256]{1,0:T(8,128)} %bitcast.2, f32[602,512]{1,0:T(8,128)} %refs_4_.1, f32[256,512]{1,0:T(8,128)} %refs_5_.1, f32[32,128,128]{2,1,0:T(8,128)} %refs_6_.1), custom_call_target="tpu_custom_call" | custom-call | tf_op jit(solution)/shard_map/pallas_call | solution.py:606
  135.9 3.1 %shard_map.95 = (f32[256,512]{1,0:T(8,128)}, f32[602,256]{1,0:T(8,128)}, f32[602,512]{1,0:T(8,128)}) custom-call(f32[256,512]{1,0:T(8,128)} %get-tuple-element.9.refs_0_, f32[602,256]{1,0:T(8,128)} %get-tuple-element.10.refs_1_, f32[602,512]{1,0:T(8,128)} %get-tuple-element.11.refs_2_), custom_call_target="tpu_custom_call" | custom-call | tf_op jit(solution)/shard_map/pallas_call | solution.py:615

commit v3 on v2

--- a/solution.py
+++ b/solution.py
@@ -18,7 +18,7 @@
 CHUNKS = 4
 SIDE = 4
 PAD = 640
-GROUPS = 19
+GROUPS = 21
 
 ROWS, COLS = 8, 64
 ROW_PREV, ROW_LAST, COL_PREV, COL_LAST = 0, SLOTS, SLOTS + ROWS, 2 * SLOTS + ROWS
@@ -54,7 +54,7 @@
         del refs[:count]
         return out
 
-    G, R0, part, zmid, zfin, GG = (take(C) for _ in range(6))
+    G, R0, part, zfin, GG = (take(C) for _ in range(5))
     m1, f1, m2, f2 = (take(C) for _ in range(4))
     gwl, sb, wa, wb, wc, gwo = (take(C) for _ in range(6))
     slots, tiles, tiles_t, w_raw, w_pad, f_raw, cot, f_hi, f_lo, ft_hi, ft_lo, prop, gf_acc, plan = take(14)
@@ -135,7 +135,7 @@
 
     loads = [
         pltpu.make_async_copy(src, dst, load_sem.at[i])
-        for i, (src, dst) in enumerate(((f_hbm, f_raw), (w_hbm, w_raw), (cot_hbm, cot), (tiles_hbm, tiles)))
+        for i, (src, dst) in enumerate(((f_hbm, f_raw), (w_hbm, w_raw), (cot_hbm, cot), (tiles_hbm, slots.at[pl.ds(0, SLOTS)])))
     ]
     load_f, load_w, load_cot, load_tiles = loads
     load_f.start()
@@ -202,22 +202,28 @@
         for line in (G[h].at[:, yo, p, 0], G[h].at[xo, :, p, 1]):
             send(line, line, SIB, (h, "a5"))
 
-    def chain(base):
-        def step(k, carry):
-            slots[k] = slots[k] + slots[plan[base + k]]
-            return carry
-        lax.fori_loop(0, SLOTS, step, 0)
-
-    def products(left_ref, load):
-        def step(i, carry):
-            out = []
+    def products(left_ref, load, prev):
+        def product(k):
+            both = left_ref[k]
+            return mm((both[:, :BLOCK], both[:, BLOCK:]), split(load(k)))
+
+        def add(i):
             for j in range(4):
                 k = i * 4 + j
-                out.append(mm(split(left_ref[k]), split(load(k))))
+                slots[k] = slots[k] + slots[plan[prev + k]]
+
+        def put(i, out):
             for j in range(4):
                 slots[i * 4 + j] = out[j]
+
+        def step(i, carry):
+            out = [product(i * 4 + j) for j in range(4)]
+            add(i - 1)
+            put(i, out)
             return carry
-        lax.fori_loop(0, SLOTS // 4, step, 0)
+        put(0, [product(j) for j in range(4)])
+        lax.fori_loop(1, SLOTS // 4, step, 0)
+        add(SLOTS // 4 - 1)
 
     def link_slots():
         lane = lax.broadcasted_iota(jnp.int32, (1, 128), 1)
@@ -252,7 +258,9 @@
 
     def turn_tiles():
         def turn(k, carry):
-            tiles_t[k] = tiles[k].T
+            tile = slots[k]
+            tiles[k] = jnp.concatenate(split(tile), axis=1)
+            tiles_t[k] = jnp.concatenate(split(tile.T), axis=1)
             return carry
         need(load_tiles)
         lax.fori_loop(0, SLOTS, turn, 0)
@@ -261,54 +269,47 @@
         ft_hi[...], ft_lo[...] = split(ft_pad[...])
 
     def F(h):
-        need(load_tiles)
         arrive(h, "a5")
 
         def load(k):
             c = col_ref[k]
             return G[h][c // 16, (c // 4) % 4, (c // 2) % 2, c % 2]
-        products(tiles, load)
-        chain(ROW_PREV)
+        products(tiles, load, ROW_PREV)
         for i in range(2 * SIDE):
             part[h][i // 2, i % 2] = slots[plan[ROW_LAST + i]]
 
     def Z1(h):
-        a, b = part[h], zfin[h]
-        send(a.at[zo, 0], zmid[h].at[0], ZR, (h, "z1"))
-        send(a.at[zo, 1], zmid[h].at[1], ZL, (h, "z1"))
-        send(a.at[zr, 1], b.at[0, 1], ZR, (h, "z2"))
-        send(a.at[zl, 0], b.at[1, 0], ZL, (h, "z2"))
-
-    def Z2(h):
-        a, b = part[h], zfin[h]
-        arrive(h, "z1")
-        a[zr, 0] = a[zr, 0] + zmid[h][0]
-        send(a.at[zr, 0], b.at[0, 0], ZR, (h, "z2"))
-        a[zl, 1] = a[zl, 1] + zmid[h][1]
-        send(a.at[zl, 1], b.at[1, 1], ZL, (h, "z2"))
-
-    def Z3(h):
-        arrive(h, "z2")
+        for b in range(2):
+            for d in (1, 3, 2):
+                send(part[h].at[at(z, d), b], zfin[h].at[d - 1, b], dev(dz=d), (h, "z" + str(b)))
+
+    def activate(h, b):
+        arrive(h, "z" + str(b))
         need(load_cot)
-        for b in range(2):
-            rows = pl.ds(b * BLOCK, BLOCK)
-            s = part[h][z, b] + zfin[h][0, b] + zfin[h][1, b]
-            sigma = jax.nn.sigmoid(s)
-            act[rows, cols(h)] = s * sigma
-            GG[h][z, b] = cot[rows, cols(h)] * sigma * (1.0 + s * (1.0 - sigma))
-        store(act.at[:, cols(h)], act_hbm.at[:, cols(h)])
-        own = GG[h].at[z]
+        rows = pl.ds(b * BLOCK, BLOCK)
+        s = (part[h][z, b] + zfin[h][0, b]) + (zfin[h][1, b] + zfin[h][2, b])
+        sigma = jax.nn.sigmoid(s)
+        act[rows, cols(h)] = s * sigma
+        GG[h][z, b] = cot[rows, cols(h)] * sigma * (1.0 + s * (1.0 - sigma))
+        own = GG[h].at[z, b]
         for d in (1, 3, 2):
-            send(own, own, dev(dz=d), (h, "g"))
+            send(own, own, dev(dz=d), (h, "g" + str(b)))
+        store(act.at[rows, cols(h)], act_hbm.at[rows, cols(h)])
+
+    def Z3a(h):
+        activate(h, 0)
+
+    def Z3b(h):
+        activate(h, 1)
 
     def B(h):
-        arrive(h, "g")
+        arrive(h, "g0")
+        arrive(h, "g1")
 
         def load(k):
             c = row_ref[k]
             return GG[h][c // 2, c % 2]
-        products(tiles_t, load)
-        chain(COL_PREV)
+        products(tiles_t, load, COL_PREV)
         left(h, *GATHER)
 
         def place(core, b):
@@ -435,8 +436,7 @@
     def groups(h):
         if h < C - 1:
             return [(0, PAD // 8, pl.ds(0, PAD // 8), "zxyz")]
-        n = PAD // 16
-        return [(0, n, pl.ds(0, n), "zxyz"), (4 * n, n, pl.ds(n, n), "yzxy")]
+        return [(0, 32, pl.ds(0, 32), "zxyz"), (128, 24, pl.ds(32, 24), "yzxy"), (224, 24, pl.ds(56, 24), "xyzx")]
 
     def piece(first, n, i):
         return pl.ds(pl.multiple_of(first + i * n, 8), n)
@@ -489,7 +489,7 @@
         gw[pl.ds(half, F_IN - half), cols(h)] = gwo[h][1, pl.ds(0, F_IN - half)]
         store(gw.at[:, cols(h)], gw_hbm.at[:, cols(h)])
 
-    stages = dict(P=project, A1=A1, A2=A2, A3=A3, A4=A4, A5=A5, F=F, Z1=Z1, Z2=Z2, Z3=Z3, B=B,
+    stages = dict(P=project, A1=A1, A2=A2, A3=A3, A4=A4, A5=A5, F=F, Z1=Z1, Z3a=Z3a, Z3b=Z3b, B=B,
                   R1a=R1a, R1b=R1b, R2=R2, R3=R3, R4=R4, R5=R5, GF=grad_features, W2=W2, W3=W3, W4=W4, W5=W5, W6=W6, W7=W7)
 
     alone = dict(plan=link, turn=turn_tiles, ft=split_features, drain=drain)
@@ -509,31 +509,31 @@
 
 
 ORDER = (
-    "P_0 P_1 A1_1 P_2",
-    "P_3 A1_0 A2_1 A1_2",
-    "A1_3 ft A3_1 A2_0",
-    "turn A2_2 plan A2_3",
-    "A4_1 A3_0 A3_2 A5_1",
-    "F_1 Z1_1 Z2_1 A4_0",
-    "A4_2 A3_3 Z3_1 A5_0",
-    "A5_2 F_0 Z1_0 F_2",
-    "Z1_2 B_1 Z2_0 A4_3",
-    "Z2_2 R1a_1 Z3_0 R1b_1",
-    "Z3_2 A5_3 F_3 Z1_3",
-    "R2_1 B_0 R3_1 R1a_0",
-    "Z2_3 R4_1 R1b_0 B_2",
-    "Z3_3 R2_0 R1b_2 R1a_2",
-    "R5_1 GF_1 R3_0 B_3",
-    "R2_2 R4_0 R1a_3 W2_1",
-    "R1b_3 R5_0 R3_2 GF_0",
-    "R2_3 W2_0 R4_2 W3_1",
-    "R3_3 R5_2 W4_1 GF_2",
-    "W2_2 W3_0 R4_3 R5_3",
-    "GF_3 W3_2 W2_3 W4_0",
-    "W5_1 W3_3 W4_2 W6_1",
-    "W5_0 drain W4_3 W5_2",
-    "W6_0 W5_3 W7_0 W6_2",
-    "W7_1 W6_3 W7_2 W7_3",
+    "P_0 P_2 A1_2 ft",
+    "P_1 A1_1 P_3 A2_2",
+    "A1_0 A2_1 A3_2 A1_3",
+    "plan turn A2_0 A4_2",
+    "A3_0 A2_3 A5_2 F_2",
+    "Z1_2 A4_0 A3_1 Z3a_2",
+    "A5_0 Z3b_2 F_0 Z1_0",
+    "A4_1 A3_3 B_2 Z3a_0",
+    "A5_1 Z3b_0 F_1 Z1_1",
+    "A4_3 R1a_2 R1b_2 B_0",
+    "Z3a_1 A5_3 Z3b_1 R2_2",
+    "R1b_0 R1a_0 F_3 Z1_3",
+    "R3_2 B_1 Z3a_3 R2_0",
+    "Z3b_3 R4_2 R1a_1 R1b_1",
+    "R3_0 B_3 R2_1 R5_2",
+    "GF_2 R4_0 R1a_3 R1b_3",
+    "W2_2 R3_1 R5_0 GF_0",
+    "W2_0 R2_3 R4_1 W3_0",
+    "R3_3 R5_1 R4_3 GF_1",
+    "W2_1 W4_0 W3_2 R5_3",
+    "W3_1 W2_3 W4_2 W5_0",
+    "GF_3 W3_3 W4_1 W5_2",
+    "W6_0 drain W4_3 W7_0",
+    "W5_1 W5_3 W6_2 W7_2",
+    "W6_1 W6_3 W7_1 W7_3",
 )
 
 
@@ -558,8 +558,7 @@
         vmem(4, 4, 2, 2, BLOCK, W)
         + vmem(4, 4, 2, BLOCK, W)
         + vmem(4, 2, BLOCK, W)
-        + vmem(2, BLOCK, W)
-        + vmem(2, 2, BLOCK, W)
+        + vmem(3, 2, BLOCK, W)
         + vmem(4, 2, BLOCK, W)
         + vmem(2, 2, 4, HALF, W)
         + vmem(2, 2, 4, BLOCK, W)
@@ -574,8 +573,8 @@
         + vmem(2, PAD // 2, W)
         + [
             pltpu.VMEM((SLOTS + 1, BLOCK, W), F32),
-            pltpu.VMEM((SLOTS, BLOCK, BLOCK), F32),
-            pltpu.VMEM((SLOTS, BLOCK, BLOCK), F32),
+            pltpu.VMEM((SLOTS, BLOCK, 2 * BLOCK), BF16),
+            pltpu.VMEM((SLOTS, BLOCK, 2 * BLOCK), BF16),
             pltpu.VMEM((width, hidden), F32),
             pltpu.VMEM((PAD, hidden), F32),
             pltpu.VMEM((width, nodes), F32),
@@ -593,7 +592,7 @@
             pltpu.SemaphoreType.DMA((GROUPS * C,)),
             pltpu.SemaphoreType.DMA((GROUPS * C,)),
             pltpu.SemaphoreType.DMA((4,)),
-            pltpu.SemaphoreType.DMA((2 * C + 1,)),
+            pltpu.SemaphoreType.DMA((3 * C + 1,)),
         ]
     )
     scalars = pl.BlockSpec(memory_space=pltpu.SMEM)

time: 139 us -> 134 us (0.964)
  Pallas kernels: 138 us -> 132 us
    pallas_call x1, Pallas kernels: 135 us -> 129 us  [body(): pl.pallas_call(kernel, out_shape=shapes, in_specs=[scalars] * 3 + [hbm] *...]
where the time goes in v3:
time: 134 us
  Pallas kernels  132 us (99%)
  between operations  1.45 us (1%)
    pallas_call x1, Pallas kernels, body(): pl.pallas_call(kernel, out_shape=shapes, in_specs=[scalars] * 3 + [hbm] *...  129 us
    pallas_call x1, Pallas kernels, body(): pl.pallas_call(hand_over, out_shape=shapes, in_specs=[pl.BlockSpec(memory...  3.08 us

profile of v3, /device:TPU:1, one launch (start us, length us, event | category | flops | bytes accessed | tf_op | source)
XLA Modules:
  0.0 133.6 jit_solution(16702498242152974551)
XLA Ops:
  1.3 129.1 %shard_map.94 = (f32[256,512]{1,0:T(8,128)}, f32[602,256]{1,0:T(8,128)}, f32[602,512]{1,0:T(8,128)}) custom-call(s32[32]{0:T(128)} %refs_0_.1, s32[32]{0:T(128)} %refs_1_.1, s32[1]{0:T(128)S(6)} %copy.10.refs_2_, f32[602,256]{1,0:T(8,128)} %bitcast.2, f32[602,512]{1,0:T(8,128)} %refs_4_.1, f32[256,512]{1,0:T(8,128)} %refs_5_.1, f32[32,128,128]{2,1,0:T(8,128)} %refs_6_.1), custom_call_target="tpu_custom_call" | custom-call | tf_op jit(solution)/shard_map/pallas_call | solution.py:605
  130.4 3.1 %shard_map.95 = (f32[256,512]{1,0:T(8,128)}, f32[602,256]{1,0:T(8,128)}, f32[602,512]{1,0:T(8,128)}) custom-call(f32[256,512]{1,0:T(8,128)} %get-tuple-element.9.refs_0_, f32[602,256]{1,0:T(8,128)} %get-tuple-element.10.refs_1_, f32[602,512]{1,0:T(8,128)} %get-tuple-element.11.refs_2_), custom_call_target="tpu_custom_call" | custom-call | tf_op jit(solution)/shard_map/pallas_call | solution.py:614

commit v4 on v3

--- a/solution.py
+++ b/solution.py
@@ -24,7 +24,8 @@
 ROW_PREV, ROW_LAST, COL_PREV, COL_LAST = 0, SLOTS, SLOTS + ROWS, 2 * SLOTS + ROWS
 
 LO, HI = pl.ds(0, HALF), pl.ds(HALF, HALF)
-GATHER = ("a1", "a2", "a3", "a4", "a5")
+POOLS = (("a1", "a2", "a3", "a4"), ("a5",), ("z0", "z1", "g0", "g1", "m2", "f2"), ("s0", "s1"), ("m1", "f1"),
+         ("w1", "w2", "w3", "w4", "w5", "w6"))
 
 
 def split(value):
@@ -96,7 +97,7 @@
 
     names = [[] for _ in range(C)]
     lines = {}
-    leaving = []
+    gone = {}
 
     def spot(group):
         chunk, name = group
@@ -104,42 +105,54 @@
             names[chunk].append(name)
         return GROUPS * chunk + names[chunk].index(name)
 
+    def pool(group):
+        chunk, name = group
+        return len(POOLS) * chunk + [name in names_of for names_of in POOLS].index(True)
+
     def send(src, dst, device, group):
         copy = pltpu.make_async_remote_copy(
-            src_ref=src, dst_ref=dst, send_sem=send_sem.at[spot(group)], recv_sem=recv_sem.at[spot(group)],
+            src_ref=src, dst_ref=dst, send_sem=send_sem.at[pool(group)], recv_sem=recv_sem.at[spot(group)],
             device_id=device, device_id_type=MESH)
         copy.start()
-        if group not in lines:
-            lines[group] = 0
-            leaving.append(group)
-        lines[group] += math.prod(src.shape) // W
-
-    def all_of(group):
-        count = lines[group]
-        ref = slots.at[pl.ds(0, count // BLOCK)] if count % BLOCK == 0 else sb[0].at[pl.ds(0, count)]
+        count = math.prod(src.shape) // W
+        lines[group] = lines.get(group, 0) + count
+        gone[pool(group)] = gone.get(pool(group), 0) + count
+
+    def all_of(count, sent, received):
+        blocks = count // BLOCK
+        if blocks * BLOCK == count:
+            ref = slots.at[pl.ds(0, blocks)]
+        elif count <= PAD // 2:
+            ref = sb[0].at[pl.ds(0, count)]
+        else:
+            ref = w_pad.at[pl.ds(0, count // C)]
         return pltpu.make_async_remote_copy(
-            src_ref=ref, dst_ref=ref, send_sem=send_sem.at[spot(group)], recv_sem=recv_sem.at[spot(group)],
+            src_ref=ref, dst_ref=ref, send_sem=send_sem.at[sent], recv_sem=recv_sem.at[received],
             device_id=XR, device_id_type=MESH)
 
     def arrive(*group):
-        all_of(group).wait_recv()
+        all_of(lines[group], pool(group), spot(group)).wait_recv()
 
     def left(h, *which):
-        for name in which:
-            all_of((h, name)).wait_send()
-            leaving.remove((h, name))
+        for number in which:
+            i = len(POOLS) * h + number
+            all_of(gone[i], i, 0).wait_send()
 
     def drain():
-        for group in list(leaving):
-            left(*group)
+        for h in range(C):
+            left(h, 2, 3, 4)
 
     loads = [
         pltpu.make_async_copy(src, dst, load_sem.at[i])
-        for i, (src, dst) in enumerate(((f_hbm, f_raw), (w_hbm, w_raw), (cot_hbm, cot), (tiles_hbm, slots.at[pl.ds(0, SLOTS)])))
+        for i, (src, dst) in enumerate(
+            [(f_hbm, f_raw), (cot_hbm, cot), (tiles_hbm, slots.at[pl.ds(0, SLOTS)])]
+            + [(w_hbm.at[:, pl.ds(h * W, W)], w_raw.at[:, pl.ds(h * W, W)]) for h in range(C)])
     ]
-    load_f, load_w, load_cot, load_tiles = loads
+    load_f, load_cot, load_tiles = loads[:3]
+    load_w = loads[3:]
     load_f.start()
-    load_w.start()
+    for load in load_w:
+        load.start()
 
     barrier = pltpu.get_barrier_semaphore()
     peers = [dev(dx=d) for d in (1, 2, 3)] + [dev(dy=d) for d in (1, 2, 3)] + [dev(dz=d) for d in (1, 2, 3)] + [SIB]
@@ -153,14 +166,14 @@
     ft_pad[pl.ds(tail, PAD - tail), :] = jnp.zeros((PAD - tail, ft_pad.shape[1]), F32)
     ft_pad[pl.ds(0, F_IN), :] = f_raw[...]
     f_hi[...], f_lo[...] = split(ft_pad[...].T)
-    load_w.wait()
-    w_pad[pl.ds(tail, PAD - tail), :] = jnp.zeros((PAD - tail, w_pad.shape[1]), F32)
-    w_pad[pl.ds(0, F_IN), :] = w_raw[...]
 
     def cols(h):
         return pl.ds(h * W, W)
 
     def project(h):
+        need(load_w[h])
+        w_pad[pl.ds(tail, PAD - tail), cols(h)] = jnp.zeros((PAD - tail, W), F32)
+        w_pad[pl.ds(0, F_IN), cols(h)] = w_raw[:, cols(h)]
         out = mm((f_hi[...], f_lo[...]), split(w_pad[:, cols(h)]))
         G[h][x, y, p, 0] = out[:BLOCK]
         G[h][x, y, p, 1] = out[BLOCK:]
@@ -263,7 +276,7 @@
             tiles_t[k] = jnp.concatenate(split(tile.T), axis=1)
             return carry
         need(load_tiles)
-        lax.fori_loop(0, SLOTS, turn, 0)
+        lax.fori_loop(0, SLOTS, turn, 0, unroll=4)
 
     def split_features():
         ft_hi[...], ft_lo[...] = split(ft_pad[...])
@@ -310,7 +323,7 @@
             c = row_ref[k]
             return GG[h][c // 2, c % 2]
         products(tiles_t, load, COL_PREV)
-        left(h, *GATHER)
+        left(h, 0, 1)
 
         def place(core, b):
             def step(i, carry):
@@ -332,7 +345,7 @@
         def add(i, carry):
             s[i // 4, i % 4, b] = s[i // 4, i % 4, b] + G[h][i // 4, i % 4, p, b]
             return carry
-        lax.fori_loop(0, 16, add, 0)
+        lax.fori_loop(0, 16, add, 0, unroll=4)
 
     def R1a(h):
         with_own(h, 0)
@@ -503,37 +516,38 @@
         else:
             stage, h = name.split("_")
             stages[stage](int(h))
-    drain()
+    for h in range(C):
+        left(h, 5)
     for copy in stores:
         copy.wait()
 
 
 ORDER = (
-    "P_0 P_2 A1_2 ft",
-    "P_1 A1_1 P_3 A2_2",
-    "A1_0 A2_1 A3_2 A1_3",
-    "plan turn A2_0 A4_2",
-    "A3_0 A2_3 A5_2 F_2",
-    "Z1_2 A4_0 A3_1 Z3a_2",
-    "A5_0 Z3b_2 F_0 Z1_0",
-    "A4_1 A3_3 B_2 Z3a_0",
-    "A5_1 Z3b_0 F_1 Z1_1",
-    "A4_3 R1a_2 R1b_2 B_0",
-    "Z3a_1 A5_3 Z3b_1 R2_2",
-    "R1b_0 R1a_0 F_3 Z1_3",
-    "R3_2 B_1 Z3a_3 R2_0",
-    "Z3b_3 R4_2 R1a_1 R1b_1",
-    "R3_0 B_3 R2_1 R5_2",
-    "GF_2 R4_0 R1a_3 R1b_3",
-    "W2_2 R3_1 R5_0 GF_0",
-    "W2_0 R2_3 R4_1 W3_0",
-    "R3_3 R5_1 R4_3 GF_1",
-    "W2_1 W4_0 W3_2 R5_3",
-    "W3_1 W2_3 W4_2 W5_0",
-    "GF_3 W3_3 W4_1 W5_2",
-    "W6_0 drain W4_3 W7_0",
-    "W5_1 W5_3 W6_2 W7_2",
-    "W6_1 W6_3 W7_1 W7_3",
+    "P_0 A1_0 P_1 ft",
+    "A1_1 P_2 P_3 turn",
+    "A2_0 A1_2 A3_0 A2_1",
+    "plan A2_2 A4_0 A3_1",
+    "A5_0 A1_3 F_0 Z1_0",
+    "A4_1 A3_2 Z3a_0 A5_1",
+    "A2_3 Z3b_0 F_1 Z1_1",
+    "A4_2 A3_3 B_0 Z3a_1",
+    "A5_2 Z3b_1 F_2 Z1_2",
+    "A4_3 R1b_0 R1a_0 B_1",
+    "A5_3 Z3a_2 Z3b_2 R2_0",
+    "R1a_1 R1b_1 F_3 Z1_3",
+    "B_2 R3_0 R2_1 Z3a_3",
+    "Z3b_3 R4_0 R1a_2 R1b_2",
+    "R3_1 R5_0 B_3 R2_2",
+    "W2_0 R4_1 GF_0 R1a_3",
+    "R1b_3 R3_2 R5_1 GF_1",
+    "W2_1 R2_3 W3_0 R4_2",
+    "R3_3 W3_1 R5_2 W4_0",
+    "W2_2 R5_3 W2_3 W3_2",
+    "W4_1 W5_0 GF_2 W3_3",
+    "W4_2 W5_1 drain W4_3",
+    "W5_2 W6_1 GF_3 R4_3",
+    "W5_3 W7_1 W6_2 W6_0",
+    "W6_3 W7_2 W7_0 W7_3",
 )
 
 
@@ -589,9 +603,9 @@
             pltpu.VMEM((nodes, hidden), F32),
             pltpu.VMEM((width, nodes), F32),
             pltpu.VMEM((width, hidden), F32),
+            pltpu.SemaphoreType.DMA((len(POOLS) * C,)),
             pltpu.SemaphoreType.DMA((GROUPS * C,)),
-            pltpu.SemaphoreType.DMA((GROUPS * C,)),
-            pltpu.SemaphoreType.DMA((4,)),
+            pltpu.SemaphoreType.DMA((3 + C,)),
             pltpu.SemaphoreType.DMA((3 * C + 1,)),
         ]
     )

time: 134 us -> 131 us (0.978)
  Pallas kernels: 132 us -> 130 us
    pallas_call x1, Pallas kernels: 129 us -> 127 us  [body(): pl.pallas_call(kernel, out_shape=shapes, in_specs=[scalars] * 3 + [hbm] *...]
where the time goes in v4:
time: 131 us
  Pallas kernels  130 us (99%)
    pallas_call x1, Pallas kernels, body(): pl.pallas_call(kernel, out_shape=shapes, in_specs=[scalars] * 3 + [hbm] *...  127 us
    pallas_call x1, Pallas kernels, body(): pl.pallas_call(hand_over, out_shape=shapes, in_specs=[pl.BlockSpec(memory...  3.08 us

profile of v4, /device:TPU:1, one launch (start us, length us, event | category | flops | bytes accessed | tf_op | source)
XLA Modules:
  0.0 131.1 jit_solution(17860267549297100689)
XLA Ops:
  1.3 126.7 %shard_map.94 = (f32[256,512]{1,0:T(8,128)}, f32[602,256]{1,0:T(8,128)}, f32[602,512]{1,0:T(8,128)}) custom-call(s32[32]{0:T(128)} %refs_0_.1, s32[32]{0:T(128)} %refs_1_.1, s32[1]{0:T(128)S(6)} %copy.10.refs_2_, f32[602,256]{1,0:T(8,128)} %bitcast.2, f32[602,512]{1,0:T(8,128)} %refs_4_.1, f32[256,512]{1,0:T(8,128)} %refs_5_.1, f32[32,128,128]{2,1,0:T(8,128)} %refs_6_.1), custom_call_target="tpu_custom_call" | custom-call | tf_op jit(solution)/shard_map/pallas_call | solution.py:619
  128.0 3.1 %shard_map.95 = (f32[256,512]{1,0:T(8,128)}, f32[602,256]{1,0:T(8,128)}, f32[602,512]{1,0:T(8,128)}) custom-call(f32[256,512]{1,0:T(8,128)} %get-tuple-element.9.refs_0_, f32[602,256]{1,0:T(8,128)} %get-tuple-element.10.refs_1_, f32[602,512]{1,0:T(8,128)} %get-tuple-element.11.refs_2_), custom_call_target="tpu_custom_call" | custom-call | tf_op jit(solution)/shard_map/pallas_call | solution.py:628

commit v5 on v4

--- a/solution.py
+++ b/solution.py
@@ -552,11 +552,26 @@
 
 
 def hand_over(*refs):
-    copies = [pltpu.make_async_copy(refs[i], refs[3 + i], refs[6].at[i]) for i in range(3)]
-    for copy in copies:
-        copy.start()
-    for copy in copies:
-        copy.wait()
+    arrays, results, held, load_sem, store_sem = refs[:3], refs[3:6], refs[6:9], refs[9], refs[10]
+    pieces = []
+    for i, axis in ((2, 1), (1, 1), (0, 0)):
+        size = arrays[i].shape[axis] // 2
+        for j in range(2):
+            part = pl.ds(j * size, size)
+            pieces.append((i, (slice(None), part) if axis else (part, slice(None))))
+    loads = [
+        pltpu.make_async_copy(arrays[i].at[place], held[i].at[place], load_sem.at[n])
+        for n, (i, place) in enumerate(pieces)]
+    stores = [
+        pltpu.make_async_copy(held[i].at[place], results[i].at[place], store_sem.at[n])
+        for n, (i, place) in enumerate(pieces)]
+    for load in loads:
+        load.start()
+    for load, store in zip(loads, stores):
+        load.wait()
+        store.start()
+    for store in stores:
+        store.wait()
 
 
 def body(features, weight, cotangent, tile_values, tile_row, tile_col, tile_count):
@@ -628,9 +643,10 @@
     activated, grad_features, grad_weight = pl.pallas_call(
         hand_over,
         out_shape=shapes,
-        in_specs=[pl.BlockSpec(memory_space=pltpu.VMEM)] * 3,
+        in_specs=[hbm] * 3,
         out_specs=(hbm,) * 3,
-        scratch_shapes=[pltpu.SemaphoreType.DMA((3,))],
+        scratch_shapes=[pltpu.VMEM(shape.shape, F32) for shape in shapes] + [pltpu.SemaphoreType.DMA((6,))] * 2,
+        compiler_params=pltpu.CompilerParams(vmem_limit_bytes=62 * 1024 * 1024),
     )(*results)
     return activated, grad_features.T, grad_weight
 

time: 131 us -> 131 us (level)
  no operation moved by 1% of the time
where the time goes in v5:
time: 131 us
  Pallas kernels  129 us (98%)
    pallas_call x1, Pallas kernels, body(): pl.pallas_call(kernel, out_shape=shapes, in_specs=[scalars] * 3 + [hbm] *...  127 us

profile of v5, /device:TPU:1, one launch (start us, length us, event | category | flops | bytes accessed | tf_op | source)
XLA Modules:
  0.0 130.6 jit_solution(92437841163997574)
XLA Ops:
  1.3 126.7 %shard_map.94 = (f32[256,512]{1,0:T(8,128)}, f32[602,256]{1,0:T(8,128)}, f32[602,512]{1,0:T(8,128)}) custom-call(s32[32]{0:T(128)} %refs_0_.1, s32[32]{0:T(128)} %refs_1_.1, s32[1]{0:T(128)S(6)} %copy.10.refs_2_, f32[602,256]{1,0:T(8,128)} %bitcast.2, f32[602,512]{1,0:T(8,128)} %refs_4_.1, f32[256,512]{1,0:T(8,128)} %refs_5_.1, f32[32,128,128]{2,1,0:T(8,128)} %refs_6_.1), custom_call_target="tpu_custom_call" | custom-call | tf_op jit(solution)/shard_map/pallas_call | solution.py:634
  128.0 2.6 %shard_map.95 = (f32[256,512]{1,0:T(8,128)}, f32[602,256]{1,0:T(8,128)}, f32[602,512]{1,0:T(8,128)}) custom-call(f32[256,512]{1,0:T(8,128)} %get-tuple-element.9.refs_0_, f32[602,256]{1,0:T(8,128)} %get-tuple-element.10.refs_1_, f32[602,512]{1,0:T(8,128)} %get-tuple-element.11.refs_2_), custom_call_target="tpu_custom_call" | custom-call | tf_op jit(solution)/shard_map/pallas_call | solution.py:643
